TPU v7x, 512 devices: a whole 4x4x16 slice. The times are simulated.
512 devices in a mesh: items: 64 (over x, z_hi, y), codes: 8 (over z_lo, core).
Axes of the slice: x: 4, y: 4, z: 16 (z_hi: 4, z_lo: 4; z = z_hi * 4 + z_lo), core: 2. Of those that a mesh axis runs over, the one named last changes fastest.
Arguments:
- block_two: bfloat16 [65536, 1024], P('items'), may hold values from -16 to 16
- block_one: bfloat16 [65536, 1024], P('items'), may hold values from -16 to 16
- codebook_two: bfloat16 [8192, 1024], P('codes', 'items'), may hold values from -6 to 6
- codebook_one: bfloat16 [8192, 1024], P('codes', 'items'), may hold values from -6 to 6
Outputs:
- rebuilt: bfloat16 [65536, 1024], P('items', 'codes')
- next_log_scale: float32 [8192], P('codes')
All inputs are finite; a program needn't handle non-finite values.
Results may differ from a plain program's by a relative error of at most 0.015.
Values may be sent and summed in bfloat16 or wider, within the bound.
No kernel may reach another device: no remote copies, remote signals or barrier semaphores. Data moves between devices by JAX's collectives and lax.ppermute only.
A program may use at most 64 MiB of HBM per device.

v0:
```python
import math

import jax
import jax.numpy as jnp
from jax import lax
from jax.sharding import PartitionSpec as P

SWEEPS = 3


def contract(left_rows, right_rows):
    return lax.dot_general(
        left_rows, right_rows, (((1,), (1,)), ((), ())), preferred_element_type=jnp.float32
    )


def make_kernel(block, full_book, inv_root):
    scores = contract(block, full_book)
    squares = jnp.sum(jnp.square(full_book.astype(jnp.float32)), axis=1)
    return jnp.exp((scores - 0.5 * squares[None, :]) * inv_root)


def row_total(kernel, scale):
    return lax.psum(jnp.dot(kernel, scale, precision=lax.Precision.HIGHEST), "codes")


def column_total(weights, kernel):
    return lax.psum(jnp.dot(weights, kernel, precision=lax.Precision.HIGHEST), "items")


def shards(block_two, block_one, codebook_two, codebook_one):
    row_count = block_two.shape[0]
    feature_count = block_two.shape[1]
    codes_here = codebook_two.shape[0]
    code_groups = lax.axis_size("codes")
    target = float(row_count * lax.axis_size("items")) / float(codes_here * code_groups)
    inv_root = 1.0 / math.sqrt(feature_count)
    full_two, full_one = (
        lax.all_gather(codebook_two, "items", axis=1, tiled=True),
        lax.all_gather(codebook_one, "items", axis=1, tiled=True),
    )
    kernel_two = make_kernel(block_two, full_two, inv_root)
    kernel_one = make_kernel(block_one, full_one, inv_root)
    col_scale = jnp.ones((codes_here,), jnp.float32)
    for sweep_index in range(SWEEPS):
        row_scale = 1.0 / row_total(kernel_two, col_scale)
        col_scale = target / column_total(row_scale, kernel_two)
    row_scale = 1.0 / row_total(kernel_two, col_scale)
    transport = (row_scale[:, None] * kernel_two * col_scale[None, :]).astype(jnp.bfloat16)
    partial_value = jnp.dot(transport, full_two, preferred_element_type=jnp.float32)
    partial_term = lax.optimization_barrier(partial_value.astype(jnp.bfloat16)).astype(jnp.float32)
    summed = lax.psum(partial_term.astype(jnp.bfloat16), "codes").astype(jnp.float32)
    share_width = feature_count // code_groups
    rebuilt = lax.dynamic_slice_in_dim(
        summed, lax.axis_index("codes") * share_width, share_width, 1
    )
    weights_one = 1.0 / lax.psum(jnp.sum(kernel_one, axis=1), "codes")
    cols_one = lax.psum(jnp.dot(weights_one, kernel_one, precision=lax.Precision.HIGHEST), "items")
    next_log_scale = math.log(target) - jnp.log(cols_one)
    return (rebuilt.astype(jnp.bfloat16), next_log_scale)


def solution(mesh):
    placed = (P("items", None), P("items", None), P("codes", "items"), P("codes", "items"))
    return jax.shard_map(
        shards,
        mesh=mesh,
        in_specs=placed,
        out_specs=(P("items", "codes"), P("codes")),
        check_vma=False,
    )
```

profile of v0, /device:TPU:1, one launch (start us, length us, event | category | flops | bytes accessed | tf_op | source)
XLA Modules:
  0.0 1097.0 jit_solution(12780915366237314931)
XLA Ops:
  8.7 121.8 %all-gather.5.cloned.1.call-done = bf16[1024,1024]{0,1:T(8,128)(2,1)} async-done(((bf16[1024,16]{0,1:T(8,128)(2,1)}), bf16[1024,1024]{0,1:T(8,128)(2,1)}) %all-gather.5.cloned.1.call-update) | async-done | bytes 2097168 | tf_op jit(solution)/shard_map/all_gather | solution.py:40
  130.5 2.1 multiply_reduce_fusion
  132.6 111.5 %all-gather.3.cloned.1.call-done = bf16[1024,1024]{0,1:T(8,128)(2,1)} async-done(((bf16[1024,16]{0,1:T(8,128)(2,1)}), bf16[1024,1024]{0,1:T(8,128)(2,1)}) %all-gather.3.cloned.1.call-update) | async-done | bytes 2097168 | tf_op jit(solution)/shard_map/all_gather | solution.py:39
  244.1 2.1 multiply_reduce_fusion.1
  246.1 4.6 multiply_exponential_fusion.1
  250.8 1.9 copy-done.1
  252.7 3.6 fusion.8
  256.3 15.8 %psum.70 = f32[1024]{0:T(1024)S(1)} all-reduce(f32[1024]{0:T(1024)S(1)} %bitcast.35), channel_id=1, replica_groups=mesh['items'=64,'codes'=8] {'codes'}, use_global_device_ids=true, to_apply=%region_1.0 | all-reduce | flops 1024 | bytes 8192 | tf_op jit(solution)/shard_map/psum | solution.py:24
  272.1 4.3 fusion.12
  276.4 194.6 %psum.71 = f32[1024]{0:T(1024)S(1)} all-reduce(f32[1024]{0:T(1024)S(1)} %bitcast.41), channel_id=1, replica_groups=mesh['items'=64,'codes'=8] {'items'}, use_global_device_ids=true, to_apply=%region_2.0 | all-reduce | flops 1024 | bytes 8192 | tf_op jit(solution)/shard_map/psum | solution.py:28
  471.0 5.8 fusion.13
  476.7 41.7 %psum.72 = f32[1024]{0:T(1024)S(1)} all-reduce(f32[1024]{0:T(1024)S(1)} %bitcast.43), channel_id=1, replica_groups=mesh['items'=64,'codes'=8] {'codes'}, use_global_device_ids=true, to_apply=%region_3.0 | all-reduce | flops 1024 | bytes 8192 | tf_op jit(solution)/shard_map/psum | solution.py:24
  518.4 4.3 fusion.14
  522.7 187.2 %psum.73 = f32[1024]{0:T(1024)S(1)} all-reduce(f32[1024]{0:T(1024)S(1)} %bitcast.45), channel_id=1, replica_groups=mesh['items'=64,'codes'=8] {'items'}, use_global_device_ids=true, to_apply=%region_4.0 | all-reduce | flops 1024 | bytes 8192 | tf_op jit(solution)/shard_map/psum | solution.py:28
  709.9 5.9 fusion.15
  715.8 4.4 fusion.1
  720.2 41.4 %all-reduce.1 = (f32[1024]{0:T(1024)S(1)}, f32[1024]{0:T(1024)S(1)}) all-reduce(f32[1024]{0:T(1024)S(1)} %bitcast.39, f32[1024]{0:T(1024)S(1)} %get-tuple-element.6), channel_id=1, replica_groups=mesh['items'=64,'codes'=8] {'codes'}, use_global_device_ids=true, to_apply=%region_5.0 | all-reduce | flops 2048 | bytes 16384 | tf_op jit(solution)/shard_map/psum | solution.py:24
  761.7 4.4 fusion.16
  766.1 2.6 fusion
  768.7 192.0 %all-reduce = (f32[1024]{0:T(1024)S(1)}, f32[1024]{0:T(1024)S(1)}) all-reduce(f32[1024]{0:T(1024)S(1)} %bitcast.37, f32[1024]{0:T(1024)S(1)} %bitcast.34), channel_id=1, replica_groups=mesh['items'=64,'codes'=8] {'items'}, use_global_device_ids=true, to_apply=%region_6.0 | all-reduce | flops 2048 | bytes 16384 | tf_op jit(solution)/shard_map/psum | solution.py:28
  960.6 5.8 fusion.17
  966.4 41.1 %psum.76 = f32[1024]{0:T(1024)S(1)} all-reduce(f32[1024]{0:T(1024)S(1)} %bitcast.47), channel_id=1, replica_groups=mesh['items'=64,'codes'=8] {'codes'}, use_global_device_ids=true, to_apply=%region_7.0 | all-reduce | flops 1024 | bytes 8192 | tf_op jit(solution)/shard_map/psum | solution.py:24
  1007.5 6.6 fusion.7
  1014.7 74.1 %all-reduce.4.cloned.1.call-done = bf16[1024,1024]{1,0:T(8,128)(2,1)} async-done(((bf16[1024,1024]{1,0:T(8,128)(2,1)}), bf16[1024,1024]{1,0:T(8,128)(2,1)}) %all-reduce.4.cloned.1.call-update) | async-done | bytes 2097168 | tf_op jit(solution)/shard_map/psum | solution.py:52
  (24 shorter events, 3.9 us)
Async XLA Ops:
  7.2 708.6 %copy-start = (bf16[1024,1024]{1,0:T(8,128)(2,1)S(1)}, bf16[1024,1024]{1,0:T(8,128)(2,1)}, u32[]{:S(2)}) copy-start(bf16[1024,1024]{1,0:T(8,128)(2,1)} %param.5) | copy-start | bytes 6291460
  7.2 123.3 %all-gather.5.cloned.1.call-start = ((), (), s32[]{:S(2)}) async-start(), calls=%async_computation.2 | async-start | bytes 2129920 | tf_op jit(solution)/shard_map/all_gather | solution.py:40
  7.9 236.2 %all-gather.3.cloned.1.call-start = ((), (), s32[]{:S(2)}) async-start(), calls=%async_computation | async-start | bytes 2129920 | tf_op jit(solution)/shard_map/all_gather | solution.py:39
  8.7 1080.2 %all-reduce.4.cloned.1.call-start = ((), (), s32[]{:S(2)}) async-start(), calls=%async_computation.1 | async-start | bytes 4194304 | tf_op jit(solution)/shard_map/psum | solution.py:52
  250.7 1.9 copy-start.1
  709.9 5.9 copy-start.3
  761.7 4.4 copy-start.2
Sparse Core Ops, SparseCore 0:
  12.2 118.2 all-gather.4
  134.7 109.3 all-gather.2
  1014.3 74.5 all-reduce.3
where the time goes:
time: 1100 us
  blocking collectives  714 us (65%)
  waiting for transfers between devices  309 us (28%)
  matrix products  52.2 us (5%)
  between operations  13.8 us (1%)
    psum x3, blocking collectives, column_total(): lax.psum(jnp.dot(weights, kernel, precision=lax.Precision.HIGHEST), 'items')  574 us
    psum x4, blocking collectives, row_total(): lax.psum(jnp.dot(kernel, scale, precision=lax.Precision.HIGHEST), 'codes')  140 us
    all_gather x1, waiting for transfers between devices, shards(): lax.all_gather(codebook_one, 'items', axis=1, tiled=True)  122 us
    all_gather x1, waiting for transfers between devices, shards(): lax.all_gather(codebook_two, 'items', axis=1, tiled=True)  112 us
    psum x1, waiting for transfers between devices, shards(): lax.psum(partial_term.astype(jnp.bfloat16), 'codes').astype(jnp.float32)  74.1 us
  transfers between devices with their start and end apart: 3, of which 3 were waited for; matrix products, arithmetic and copies ran while one was open for 0% of the time, Pallas kernels for 0%

commit v1 on v0

v1 whole, which is shorter than its diff:
```python
import functools
import math

import jax
import jax.numpy as jnp
from jax import lax
from jax.experimental import pallas as pl
from jax.experimental.pallas import tpu as pltpu
from jax.sharding import PartitionSpec as P

SWEEPS = 3
RING = 4
PLANE = ("x", "y")
CODES = ("z_lo", "core")
ITEMS = ("x", "z_hi", "y")
MIB = 1 << 20
STEP = 256
MOST = 48 * MIB
HBM = pl.BlockSpec(memory_space=pltpu.HBM)
FULL = pl.BlockSpec(memory_space=pltpu.VMEM)
BF16 = jnp.bfloat16
F32 = jnp.float32


def call(body, outs, name, ins, flops=0, nbytes=4 * MIB, limit=16 * MIB, scratch=(), out_specs=None):
    ins = [i if isinstance(i, tuple) else (i, FULL) for i in ins]
    specs = {} if out_specs is None else {"out_specs": out_specs}
    return pl.pallas_call(
        body,
        out_shape=outs,
        in_specs=[spec for _, spec in ins],
        scratch_shapes=list(scratch),
        compiler_params=pltpu.CompilerParams(vmem_limit_bytes=limit),
        cost_estimate=pl.CostEstimate(flops=flops, bytes_accessed=nbytes, transcendentals=0),
        name=name,
        **specs,
    )(*[array for array, _ in ins])


def shape(*sizes, of=F32):
    return jax.ShapeDtypeStruct(sizes, of)


def spread(rows, count):
    return jnp.broadcast_to(rows[None], (count,) + rows.shape)


def nt(a, b):
    return lax.dot_general(a, b, (((1,), (1,)), ((), ())), preferred_element_type=F32)


def nn(a, b):
    return jnp.dot(a, b, preferred_element_type=F32)


def k_rows(block, book, norms, inv_root):
    scores = nn(block, book)
    return jnp.exp((scores - norms) * inv_root).astype(BF16)


def fan_body(copies, column, two, one):
    run = column.shape[1] // 2
    for z in range(column.shape[0]):
        one[z] = column[z, run:, :]
        for i in range(copies):
            two[i, z] = column[z, :run, :]


def fetch_book(came, book, sems):
    fetches = []
    for x in range(RING):
        for y in range(RING):
            move = pltpu.make_async_copy(came.at[x * RING + y], book.at[x, :, y], sems.at[x * RING + y])
            move.start()
            fetches.append(move)
    return fetches


def half_norms(book, fetches):
    acc = jnp.zeros(book.shape[3:], F32)
    for x in range(RING):
        for y in range(RING):
            fetches[x * RING + y].wait()
            for z in range(RING):
                wide = book[x, z, y].astype(F32)
                acc = acc + wide * wide
    return 0.5 * jnp.sum(acc, axis=0, keepdims=True)


def make_k(inv_root, groups, came, block, k, total, book, held, sems, after_step=None):
    rows, features = block.shape
    codes = book.shape[-1]
    fetches = fetch_book(came, book, sems)
    loads = []
    for i in range(rows // STEP):
        here = pl.ds(i * STEP, STEP)
        loads.append(pltpu.make_async_copy(block.at[here], held.at[here], sems.at[len(fetches) + i]))
        loads[-1].start()
    norms = half_norms(book, fetches)
    ones = jnp.ones((16, codes), BF16)
    for i, load in enumerate(loads):
        here = slice(i * STEP, (i + 1) * STEP)
        load.wait()
        values = k_rows(held[here, :], book[...].reshape(features, codes), norms, inv_root)
        k[here, :] = values
        total[:, :, here] = spread(nt(ones, values)[0:1], groups)
        if after_step is not None:
            after_step(i)


def kernel_two_body(inv_root, groups, came, block, k_out, total, book, held, sems):
    make_k(inv_root, groups, came, block, k_out, total, book, held, sems)


def kernel_one_body(inv_root, groups, came, block, after, k_out, total, book, held, k, sems, saved):
    saves = []

    def save(i):
        here = pl.ds(i * STEP, STEP)
        saves.append(pltpu.make_async_copy(k.at[here], k_out.at[here], saved.at[i]))
        saves[-1].start()

    make_k(inv_root, groups, came, block, k, total, book, held, sems, save)
    for move in saves:
        move.wait()


def two_terms(row):
    high = row.astype(BF16).astype(F32)
    at = lax.broadcasted_iota(jnp.int32, (16, row.shape[1]), 0)
    return jnp.where(at == 0, high, jnp.where(at == 1, row - high, 0.0)).astype(BF16)


def over_codes(scale, k):
    return jnp.sum(nt(two_terms(scale), k[...]), axis=0, keepdims=True)


def over_items(scale, k):
    return jnp.sum(nn(two_terms(scale), k[...]), axis=0, keepdims=True)


def col_body(copies, gathered, k, col_out, scale_out):
    scale = 1.0 / jnp.sum(gathered[...], axis=0)
    scale_out[...] = scale
    col_out[...] = spread(over_items(scale, k), copies)


def both_cols_body(copies, gathered, k, k_one, col_out, scale_out, held, sem):
    fetch = pltpu.make_async_copy(k_one, held, sem)
    fetch.start()
    scale = 1.0 / jnp.sum(gathered[...], axis=0)
    scale_out[...] = scale[0:1]
    col_out[:, 0:1, :] = spread(over_items(scale[0:1], k), copies)
    fetch.wait()
    col_out[:, 1:2, :] = spread(over_items(scale[1:2], held), copies)


def row_body(target, groups, cols, k, *refs):
    out = refs[-1]
    scale = target / jnp.sum(cols[...], axis=0)[0:1]
    out[:, 0:1, :] = spread(over_codes(scale, k), groups)
    for more in refs[:-1]:
        out[:, 1:2, :] = more[...]


def halves(row):
    high = row.astype(BF16)
    return high, (row - high.astype(F32)).astype(BF16)


def cut(row, width):
    return jnp.concatenate([row[:, i : i + width] for i in range(0, row.shape[1], width)], 0)


def fetch_parity(came, picked, parity, sems):
    fetches = []
    for x in range(RING):
        for y in range(RING):
            here = came.at[x * RING + y, pl.ds(2 * parity, 2)]
            move = pltpu.make_async_copy(here, picked.at[x, :, y], sems.at[x * RING + y])
            move.start()
            fetches.append(move)
    return fetches


def transport_body(target, cols, r, k, came, t_out, other_out, sums_out, picked, sems):
    rows, codes = k.shape
    wide = other_out.shape[1]
    fetches = fetch_parity(came, picked, 1 - lax.axis_index("core"), sems)
    scale = target / jnp.sum(cols[...], axis=0)[0:1]
    sums = over_codes(scale, k)
    sums_out[...] = sums
    parts = jnp.concatenate([cut(part.astype(F32), wide) for part in halves(sums)], 0)
    filled = jnp.concatenate([parts, jnp.zeros((16 - parts.shape[0], wide), F32)], 0)
    other_out[rows : rows + 16, :] = filled.astype(BF16)
    r_up = jnp.transpose(jnp.broadcast_to(r[0:1, :], (8, r.shape[1])))
    for fetch in fetches:
        fetch.wait()
    for i in range(rows // STEP):
        here = slice(i * STEP, (i + 1) * STEP)
        t = (r_up[here, 0:1] * k[here, :].astype(F32) * scale).astype(BF16)
        t_out[here, :] = t
        other_out[here, :] = nt(t, picked[...].reshape(wide, codes)).astype(BF16)


def mine_body(t, came, out, picked, sems):
    wide = out.shape[1]
    for fetch in fetch_parity(came, picked, lax.axis_index("core"), sems):
        fetch.wait()
    for i in range(t.shape[0] // STEP):
        here = slice(i * STEP, (i + 1) * STEP)
        out[here, :] = nt(t[here, :], picked[...].reshape(wide, t.shape[1]))


def pack(sums):
    return jnp.concatenate([part.astype(F32) for part in halves(sums)], 0).astype(BF16)


def unpack(tail):
    tail = tail.astype(F32)
    return tail[:8] + tail[8:]


def pair_body(mine, came, sums, here_out, far_out, sums_out, cross_out, beside_out):
    rows, wide = mine.shape
    width = wide // RING
    tail = came[rows : rows + 16, :].astype(F32)
    n = rows // wide
    theirs = [tail[i : i + 1, :] + tail[n + i : n + i + 1, :] for i in range(n)]
    both = cut(sums[...] + jnp.concatenate(theirs, 1), width)
    sums_out[...] = both
    z = lax.axis_index("z_lo")
    pair = z + 1 - 2 * (z % 2)
    far = (z + 2) % RING
    for chip, out in ((z, here_out), (far, far_out), ((pair + 2) % RING, cross_out), (pair, beside_out)):
        lanes = pl.ds(pl.multiple_of(chip * width, width), width)
        value = mine[:, lanes] + came[:rows, lanes].astype(F32)
        out[:rows, :] = value.astype(out.dtype)
    cross_out[rows : rows + 16, :] = pack(both)


def cross_body(far, came, sums, out, sums_out):
    rows = far.shape[0]
    out[:rows, :] = (far[...] + came[:rows, :].astype(F32)).astype(BF16)
    both = sums[...] + unpack(came[rows : rows + 16, :])
    sums_out[...] = both
    out[rows : rows + 16, :] = pack(both)


def last_body(own, beside, far, sums, r, out):
    rows, width = out.shape
    total = sums[...] + unpack(far[rows : rows + 16, :])
    ratio = jnp.transpose(1.0 / (cut(r[0:1, :], width) * total))
    for i in range(rows // width):
        here = slice(i * width, (i + 1) * width)
        value = own[here, :] + beside[here, :].astype(F32) + far[here, :].astype(F32)
        out[here, :] = (value * ratio[:, i : i + 1]).astype(out.dtype)


def shards(block_two, block_one, codebook_two, codebook_one):
    rows, features = block_two.shape
    codes, run = codebook_two.shape
    groups = lax.axis_size(CODES)
    target = float(rows * lax.axis_size(ITEMS)) / float(codes * groups)
    inv_root = 1.0 / math.sqrt(features)
    book_flops = 2 * rows * features * codes

    plane = RING * RING
    sem = pltpu.SemaphoreType.DMA
    steps = rows // STEP
    both_books = spread(jnp.concatenate([codebook_two.T, codebook_one.T], 0), RING)
    column = lax.all_to_all(both_books, "z_hi", 0, 0)
    two, one = call(
        functools.partial(fan_body, plane),
        (shape(plane, RING, run, codes, of=BF16), shape(RING, run, codes, of=BF16)),
        "fan",
        [column],
    )
    came_two = lax.all_to_all(two, PLANE, 0, 0)
    came_two, one = lax.optimization_barrier((came_two, one))
    came_one = lax.all_gather(one, PLANE, axis=0, tiled=False)
    book_room = [
        pltpu.VMEM((RING, RING, RING, run, codes), BF16),
        pltpu.VMEM((rows, features), BF16),
    ]
    k_two, row_sums = call(
        functools.partial(kernel_two_body, inv_root, groups),
        (shape(rows, codes, of=BF16), shape(groups, 1, rows)),
        "kernel_two",
        [(came_two, HBM), (block_two, HBM)],
        flops=book_flops,
        limit=MOST,
        scratch=book_room + [sem((plane + steps,))],
    )

    def make_k_one(after):
        return call(
            functools.partial(kernel_one_body, inv_root, groups),
            (shape(rows, codes, of=BF16), shape(groups, 1, rows)),
            "kernel_one",
            [(came_one, HBM), (block_one, HBM), (after, HBM)],
            flops=book_flops,
            limit=MOST + 2 * MIB,
            scratch=book_room + [pltpu.VMEM((rows, codes), BF16), sem((plane + steps,)), sem((steps,))],
            out_specs=(HBM, FULL),
        )

    more = []
    small = 32 * rows * codes
    for sweep in range(SWEEPS):
        last = sweep == SWEEPS - 1
        n = 2 if last else 1
        gathered = lax.all_to_all(row_sums, CODES, 0, 0)
        outs = (shape(plane, n, codes), shape(1, rows))
        if last:
            col, scale = call(
                functools.partial(both_cols_body, plane),
                outs,
                "columns",
                [gathered, k_two, (k_one, HBM)],
                flops=small,
                limit=MOST,
                scratch=[pltpu.VMEM((rows, codes), BF16), sem],
            )
        else:
            col, scale = call(
                functools.partial(col_body, plane), outs, "columns", [gathered, k_two], flops=small
            )
        col = spread(jnp.sum(lax.all_to_all(col, PLANE, 0, 0), axis=0), RING)
        cols = lax.all_to_all(col, "z_hi", 0, 0)
        if sweep == 1:
            k_one, first_one = make_k_one(col)
            more = [first_one]
        if not last:
            row_sums = call(
                functools.partial(row_body, target, groups),
                shape(groups, 1 + len(more), rows),
                "rows",
                [cols, k_two] + more,
                flops=small,
            )

    wide = features // 2
    width = features // groups
    picked = pltpu.VMEM((RING, 2, RING, run, codes), BF16)
    t, other, sums = call(
        functools.partial(transport_body, target),
        (shape(rows, codes, of=BF16), shape(rows + 16, wide, of=BF16), shape(1, rows)),
        "transport",
        [cols, scale, k_two, (came_two, HBM)],
        flops=book_flops // 2,
        limit=MOST - 4 * MIB,
        scratch=[picked, sem((plane,))],
    )
    came = lax.ppermute(other, "core", [(0, 1), (1, 0)])
    mine = call(
        mine_body,
        shape(rows, wide),
        "mine",
        [t, (came_two, HBM)],
        flops=book_flops // 2,
        limit=MOST - 4 * MIB,
        scratch=[picked, sem((plane,))],
    )
    tall = shape(rows + 16, width, of=BF16)
    own, far, sums, cross, beside = call(
        pair_body,
        (shape(rows, width), shape(rows, width), shape(8, width), tall, shape(rows, width, of=BF16)),
        "pair",
        [mine, came, sums],
        limit=24 * MIB,
    )
    neighbours = [(0, 1), (1, 0), (2, 3), (3, 2)]
    crossed = lax.ppermute(cross, "z_lo", neighbours)
    passed, sums = call(cross_body, (tall, shape(8, width)), "cross", [far, crossed, sums])
    passed, beside = lax.optimization_barrier((passed, beside))
    passed = lax.ppermute(passed, "z_lo", [(0, 2), (2, 0), (1, 3), (3, 1)])
    beside = lax.ppermute(beside, "z_lo", neighbours)
    rebuilt = call(
        last_body, shape(rows, width, of=BF16), "last", [own, beside, passed, sums, scale]
    )
    cols_one = jnp.sum(cols[:, 1], axis=0)
    next_log_scale = math.log(target) - jnp.log(cols_one)
    return rebuilt, next_log_scale


def solution(mesh):
    sizes = (RING, RING, RING, RING, 2)
    rings = jax.sharding.Mesh(mesh.devices.reshape(sizes), ("x", "z_hi", "y", "z_lo", "core"))
    block, book = P(ITEMS, None), P(CODES, ITEMS)
    return jax.shard_map(
        shards,
        mesh=rings,
        in_specs=(block, block, book, book),
        out_specs=(P(ITEMS, CODES), P(CODES)),
        check_vma=False,
    )
```

time: 1100 us -> 246 us (0.22)
  blocking collectives: 714 us -> 162 us
  waiting for transfers between devices: 309 us -> 22.4 us
  matrix products: 52.2 us -> 0 us
  Pallas kernels: 0 us -> 23.3 us
  starting transfers between devices: 0.11 us -> 16.2 us
    psum x7 -> x0, blocking collectives: 714 us -> none  [the longest x3 574 us: column_total(): lax.psum(jnp.dot(weights, kernel, precision=lax.Precision.HIGHEST), 'items')]
    all_gather x2 -> x1, waiting for transfers between devices: 233 us -> 0.02 us  [shards(): came_one = lax.all_gather(one, PLANE, axis=0, tiled=False)]
    all_to_all x0 -> x10, blocking collectives: none -> 162 us  [the longest x3 43.4 us: shards(): gathered = lax.all_to_all(row_sums, CODES, 0, 0)]
    psum x1 -> x0, waiting for transfers between devices: 74.1 us -> none  [shards(): lax.psum(partial_term.astype(jnp.bfloat16), 'codes').astype(jnp.float32)]
    dot_general x11 -> x0, matrix products: 52.2 us -> none  [the longest x4 21 us: row_total(): jnp.dot(kernel, scale, precision=lax.Precision.HIGHEST)]
    pallas_call x0 -> x13, Pallas kernels: none -> 23.3 us  [call(): pl.pallas_call(body, out_shape=outs, in_specs=[spec for _, spec in ins],...]
    ppermute x0 -> x4, waiting for transfers between devices: none -> 18.4 us  [the longest x1 7.13 us: shards(): crossed = lax.ppermute(cross, 'z_lo', neighbours)]
    ppermute x0 -> x4, starting transfers between devices: none -> 12.9 us  [the longest x1 5.61 us: shards(): came = lax.ppermute(other, 'core', [(0, 1), (1, 0)])]
  transfers between devices with their start and end apart: 3 -> 6, of which waited for: 3 -> 5; matrix products, arithmetic and copies ran while one was open for 0% -> 1% of each run, Pallas kernels for 0% -> 7%
where the time goes in v1:
time: 246 us; the launch traced here: 245 us
  blocking collectives  162 us (66%)
  Pallas kernels  23.3 us (9%)
  waiting for transfers between devices  22.4 us (9%)
  starting transfers between devices  16.2 us (7%)
  between operations  14.2 us (6%)
  local copies, waits for them, and re-layouts  5.14 us (2%)
    all_to_all x3, blocking collectives, shards(): gathered = lax.all_to_all(row_sums, CODES, 0, 0)  43.4 us
    all_to_all x2, blocking collectives, shards(): cols = lax.all_to_all(col, 'z_hi', 0, 0)  32.4 us
    all_to_all x1, blocking collectives, shards(): column = lax.all_to_all(both_books, 'z_hi', 0, 0)  29.6 us
    all_to_all x3, blocking collectives, shards(): col = spread(jnp.sum(lax.all_to_all(col, PLANE, 0, 0), axis=0), RING)  28.6 us
    all_to_all x1, blocking collectives, shards(): came_two = lax.all_to_all(two, PLANE, 0, 0)  28.3 us
    pallas_call x13, Pallas kernels, call(): pl.pallas_call(body, out_shape=outs, in_specs=[spec for _, spec in ins],...  23.3 us
    ppermute x1, waiting for transfers between devices, shards(): crossed = lax.ppermute(cross, 'z_lo', neighbours)  7.13 us
    ppermute x1, waiting for transfers between devices, shards(): beside = lax.ppermute(beside, 'z_lo', neighbours)  6.73 us
  transfers between devices with their start and end apart: 6, of which 5 were waited for; matrix products, arithmetic and copies ran while one was open for 1% of the time, Pallas kernels for 7%

profile of v1, /device:TPU:1, one launch (start us, length us, event | category | flops | bytes accessed | tf_op | source)
XLA Modules:
  0.0 245.0 jit_solution(1513151919825027357)
XLA Ops:
  8.0 29.6 %all_to_all.55.column = bf16[4,32,1024]{2,1,0:T(8,128)(2,1)S(1)} all-to-all(bf16[4,32,1024]{2,1,0:T(8,128)(2,1)S(1)} %broadcast_in_dim.8), channel_id=1, replica_groups=mesh['x'=4,'z_hi'=4,'y'=4,'z_lo'=4,'core'=2] {'z_hi'}, dimensions={0} | all-to-all | bytes 524288 | tf_op jit(solution)/shard_map/all_to_all | solution.py:272
  38.4 28.3 %all_to_all.56.came = bf16[16,4,16,1024]{3,2,1,0:T(8,128)(2,1)} all-to-all(bf16[16,4,16,1024]{3,2,1,0:T(8,128)(2,1)S(1)} %get-tuple-element.26), channel_id=1, replica_groups=mesh['x'=4,'z_hi'=4,'y'=4,'z_lo'=4,'core'=2] {'x','y'}, dimensions={0} | all-to-all | bytes 4194304 | tf_op jit(solution)/shard_map/all_to_all | solution.py:279
  68.3 5.8 %kernel_two.1 = (bf16[1024,1024]{1,0:T(8,128)(2,1)S(1)}, f32[8,1,1024]{2,1,0:T(1,128)S(1)}) custom-call(bf16[16,4,16,1024]{3,2,1,0:T(8,128)(2,1)S(1)} %copy-done, bf16[1024,1024]{1,0:T(8,128)(2,1)} %block.2), custom_call_target="tpu_custom_call" | custom-call | flops 2147483648 | bytes 4194304 | tf_op jit(solution)/shard_map/kernel_two/pallas_call | solution.py:28
  74.1 21.8 %all_to_all.57.gathered = f32[8,1,1024]{2,1,0:T(1,128)S(1)} all-to-all(f32[8,1,1024]{2,1,0:T(1,128)S(1)} %get-tuple-element.29), channel_id=1, replica_groups=mesh['x'=4,'z_hi'=4,'y'=4,'z_lo'=4,'core'=2] {'z_lo','core'}, dimensions={0} | all-to-all | bytes 65536 | tf_op jit(solution)/shard_map/all_to_all | solution.py:313
  96.8 9.5 %all_to_all.58 = f32[16,1,1024]{2,1,0:T(1,128)S(1)} all-to-all(f32[16,1,1024]{2,1,0:T(1,128)S(1)} %get-tuple-element.31), channel_id=1, replica_groups=mesh['x'=4,'z_hi'=4,'y'=4,'z_lo'=4,'core'=2] {'x','y'}, dimensions={0} | all-to-all | bytes 131072 | tf_op jit(solution)/shard_map/all_to_all | solution.py:329
  106.3 14.5 %all_to_all.59.cols = f32[4,1,1024]{2,1,0:T(1,128)S(1)} all-to-all(f32[4,1,1024]{2,1,0:T(1,128)S(1)} %broadcast_in_dim.9), channel_id=1, replica_groups=mesh['x'=4,'z_hi'=4,'y'=4,'z_lo'=4,'core'=2] {'z_hi'}, dimensions={0} | all-to-all | bytes 32768 | tf_op jit(solution)/shard_map/all_to_all | solution.py:330
  121.5 10.8 %all_to_all.60.gathered = f32[8,1,1024]{2,1,0:T(1,128)S(1)} all-to-all(f32[8,1,1024]{2,1,0:T(1,128)S(1)} %rows.2), channel_id=1, replica_groups=mesh['x'=4,'z_hi'=4,'y'=4,'z_lo'=4,'core'=2] {'z_lo','core'}, dimensions={0} | all-to-all | bytes 65536 | tf_op jit(solution)/shard_map/all_to_all | solution.py:313
  133.3 9.4 %all_to_all.61 = f32[16,1,1024]{2,1,0:T(1,128)S(1)} all-to-all(f32[16,1,1024]{2,1,0:T(1,128)S(1)} %get-tuple-element.32), channel_id=1, replica_groups=mesh['x'=4,'z_hi'=4,'y'=4,'z_lo'=4,'core'=2] {'x','y'}, dimensions={0} | all-to-all | bytes 131072 | tf_op jit(solution)/shard_map/all_to_all | solution.py:329
  143.4 3.2 %all-to-all-start.7 = ((f32[4,1,1024]{2,1,0:T(1,128)}), f32[4,1,1024]{2,1,0:T(1,128)S(1)}, u32[]{:S(2)}, u32[]{:S(2)}) async-start(f32[4,1,1024]{2,1,0:T(1,128)} %broadcast_in_dim.10.after), calls=%async_computation.7 | async-start | bytes 32768 | tf_op jit(solution)/shard_map/all_to_all | solution.py:330
  146.6 6.0 %kernel_one.1 = (bf16[1024,1024]{1,0:T(8,128)(2,1)S(1)}, f32[8,1,1024]{2,1,0:T(1,128)S(1)}) custom-call(bf16[16,4,16,1024]{3,2,1,0:T(8,128)(2,1)} %bitcast.5, bf16[1024,1024]{1,0:T(8,128)(2,1)} %block.3, f32[4,1,1024]{2,1,0:T(1,128)} %broadcast_in_dim.10.after), custom_call_target="tpu_custom_call" | custom-call | flops 2147483648 | bytes 4194304 | tf_op jit(solution)/shard_map/kernel_one/pallas_call | solution.py:28
  154.0 4.0 %all-to-all-done.7.cols = f32[4,1,1024]{2,1,0:T(1,128)S(1)} async-done(((f32[4,1,1024]{2,1,0:T(1,128)}), f32[4,1,1024]{2,1,0:T(1,128)S(1)}, u32[]{:S(2)}, u32[]{:S(2)}) %all-to-all-start.7) | async-done | bytes 16416 | tf_op jit(solution)/shard_map/all_to_all | solution.py:330
  158.7 10.8 %all_to_all.62.gathered = f32[8,2,1024]{2,1,0:T(2,128)S(1)} all-to-all(f32[8,2,1024]{2,1,0:T(2,128)S(1)} %rows.3), channel_id=1, replica_groups=mesh['x'=4,'z_hi'=4,'y'=4,'z_lo'=4,'core'=2] {'z_lo','core'}, dimensions={0} | all-to-all | bytes 131072 | tf_op jit(solution)/shard_map/all_to_all | solution.py:313
  170.5 9.6 %all_to_all.63 = f32[16,2,1024]{2,1,0:T(2,128)S(1)} all-to-all(f32[16,2,1024]{2,1,0:T(2,128)S(1)} %get-tuple-element.36), channel_id=1, replica_groups=mesh['x'=4,'z_hi'=4,'y'=4,'z_lo'=4,'core'=2] {'x','y'}, dimensions={0} | all-to-all | bytes 262144 | tf_op jit(solution)/shard_map/all_to_all | solution.py:329
  180.2 17.8 %all_to_all.64.cols = f32[4,2,1024]{2,1,0:T(2,128)S(1)} all-to-all(f32[4,2,1024]{2,1,0:T(2,128)S(1)} %broadcast_in_dim.11), channel_id=1, replica_groups=mesh['x'=4,'z_hi'=4,'y'=4,'z_lo'=4,'core'=2] {'z_hi'}, dimensions={0} | all-to-all | bytes 65536 | tf_op jit(solution)/shard_map/all_to_all | solution.py:330
  198.0 1.6 copy-done.1
  199.6 2.9 %transport.1 = (bf16[1024,1024]{1,0:T(8,128)(2,1)S(1)}, bf16[1040,512]{1,0:T(8,128)(2,1)S(1)}, f32[1,1024]{1,0:T(1,128)S(1)}) custom-call(f32[4,2,1024]{2,1,0:T(2,128)S(1)} %all_to_all.64.cols, f32[1,1024]{1,0:T(1,128)S(1)} %get-tuple-element.37.r, bf16[1024,1024]{1,0:T(8,128)(2,1)S(1)} %get-tuple-element.30.k, bf16[16,4,16,1024]{3,2,1,0:T(8,128)(2,1)S(1)} %copy-done.1), custom_call_target="tpu_custom_call" | custom-call | flops 1073741824 | bytes 4194304 | tf_op jit(solution)/shard_map/transport/pallas_call | solution.py:28
  202.5 5.6 %collective-permute-start = (bf16[1040,512]{1,0:T(8,128)(2,1)S(1)}, bf16[1040,512]{1,0:T(8,128)(2,1)S(1)}, u32[]{:S(2)}, u32[]{:S(2)}) collective-permute-start(bf16[1040,512]{1,0:T(8,128)(2,1)S(1)} %get-tuple-element.39), channel_id=1, source_target_pairs={{0,1},{1,0},{2,3},{3,2},{4,5},{5,4},{6,7},{7,6},{8,9},{9,8},{10,11... | collective-permute-start | bytes 3194888 | tf_op jit(solution)/shard_map/ppermute | solution.py:355
  208.1 2.1 mine.1
  210.9 2.4 collective-permute-start.1
  213.2 7.1 %collective-permute-done.1.came = bf16[1040,128]{1,0:T(8,128)(2,1)S(1)} collective-permute-done((bf16[1040,128]{1,0:T(8,128)(2,1)S(1)}, bf16[1040,128]{1,0:T(8,128)(2,1)S(1)}, u32[]{:S(2)}, u32[]{:S(2)}) %collective-permute-start.1) | collective-permute-done | bytes 266272 | tf_op jit(solution)/shard_map/ppermute | solution.py:374
  220.4 2.1 collective-permute-start.3
  222.5 2.8 %collective-permute-start.2 = (bf16[1024,128]{1,0:T(8,128)(2,1)S(1)}, bf16[1024,128]{1,0:T(8,128)(2,1)S(1)}, u32[]{:S(2)}, u32[]{:S(2)}) collective-permute-start(bf16[1024,128]{1,0:T(8,128)(2,1)S(1)} %get-tuple-element.47), channel_id=1, source_target_pairs={{0,2},{2,0},{4,6},{6,4},{1,3},{3,1},{5,7},{7,5},{8,10},{10,8},{12,... | collective-permute-start | bytes 786440 | tf_op jit(solution)/shard_map/ppermute | solution.py:378
  226.0 6.7 %collective-permute-done.2.beside = bf16[1024,128]{1,0:T(8,128)(2,1)S(1)} collective-permute-done((bf16[1024,128]{1,0:T(8,128)(2,1)S(1)}, bf16[1024,128]{1,0:T(8,128)(2,1)S(1)}, u32[]{:S(2)}, u32[]{:S(2)}) %collective-permute-start.2) | collective-permute-done | bytes 262176 | tf_op jit(solution)/shard_map/ppermute | solution.py:378
  232.7 4.4 %collective-permute-done.3.far = bf16[1040,128]{1,0:T(8,128)(2,1)S(1)} collective-permute-done((bf16[1040,128]{1,0:T(8,128)(2,1)S(1)}, bf16[1040,128]{1,0:T(8,128)(2,1)S(1)}, u32[]{:S(2)}, u32[]{:S(2)}) %collective-permute-start.3) | collective-permute-done | bytes 266272 | tf_op jit(solution)/shard_map/ppermute | solution.py:377
  (30 shorter events, 11.7 us)
Async XLA Ops:
  7.2 139.5 %all-gather.3.cloned.1.call-start = ((), (), s32[]{:S(2)}) async-start(), calls=%async_computation.11 | async-start | bytes 2228224 | tf_op jit(solution)/shard_map/all_gather | solution.py:281
  66.7 1.6 copy-start
  143.4 14.7 %all-to-all-start.7 = ((f32[4,1,1024]{2,1,0:T(1,128)}), f32[4,1,1024]{2,1,0:T(1,128)S(1)}, u32[]{:S(2)}, u32[]{:S(2)}) async-start(f32[4,1,1024]{2,1,0:T(1,128)} %broadcast_in_dim.10.after), calls=%async_computation.7 | async-start | bytes 32768 | tf_op jit(solution)/shard_map/all_to_all | solution.py:330
  152.7 1.3 copy-start.2
  158.0 11.5 %copy-start.3 = (bf16[1024,1024]{1,0:T(8,128)(2,1)S(1)}, bf16[1024,1024]{1,0:T(8,128)(2,1)}, u32[]{:S(2)}) copy-start(bf16[1024,1024]{1,0:T(8,128)(2,1)} %copy-done.2) | copy-start | bytes 6291460
  198.0 1.6 copy-start.1
  202.5 7.9 %collective-permute-start = (bf16[1040,512]{1,0:T(8,128)(2,1)S(1)}, bf16[1040,512]{1,0:T(8,128)(2,1)S(1)}, u32[]{:S(2)}, u32[]{:S(2)}) collective-permute-start(bf16[1040,512]{1,0:T(8,128)(2,1)S(1)} %get-tuple-element.39), channel_id=1, source_target_pairs={{0,1},{1,0},{2,3},{3,2},{4,5},{5,4},{6,7},{7,6},{8,9},{9,8},{10,11... | collective-permute-start | bytes 3194888 | tf_op jit(solution)/shard_map/ppermute | solution.py:355
  210.9 9.5 %collective-permute-start.1 = (bf16[1040,128]{1,0:T(8,128)(2,1)S(1)}, bf16[1040,128]{1,0:T(8,128)(2,1)S(1)}, u32[]{:S(2)}, u32[]{:S(2)}) collective-permute-start(bf16[1040,128]{1,0:T(8,128)(2,1)S(1)} %get-tuple-element.43), channel_id=1, source_target_pairs={{0,2},{2,0},{4,6},{6,4},{1,3},{3,1},{5,7},{7,5},{8,10},{10,8},{12,... | collective-permute-start | bytes 798728 | tf_op jit(solution)/shard_map/ppermute | solution.py:374
  220.4 16.7 %collective-permute-start.3 = (bf16[1040,128]{1,0:T(8,128)(2,1)S(1)}, bf16[1040,128]{1,0:T(8,128)(2,1)S(1)}, u32[]{:S(2)}, u32[]{:S(2)}) collective-permute-start(bf16[1040,128]{1,0:T(8,128)(2,1)S(1)} %get-tuple-element.48), channel_id=1, source_target_pairs={{0,4},{4,0},{2,6},{6,2},{1,5},{5,1},{3,7},{7,3},{8,12},{12,8},{10,... | collective-permute-start | bytes 798728 | tf_op jit(solution)/shard_map/ppermute | solution.py:377
  222.5 10.2 %collective-permute-start.2 = (bf16[1024,128]{1,0:T(8,128)(2,1)S(1)}, bf16[1024,128]{1,0:T(8,128)(2,1)S(1)}, u32[]{:S(2)}, u32[]{:S(2)}) collective-permute-start(bf16[1024,128]{1,0:T(8,128)(2,1)S(1)} %get-tuple-element.47), channel_id=1, source_target_pairs={{0,2},{2,0},{4,6},{6,4},{1,3},{3,1},{5,7},{7,5},{8,10},{10,8},{12,... | collective-permute-start | bytes 786440 | tf_op jit(solution)/shard_map/ppermute | solution.py:378
Sparse Core Ops, SparseCore 0:
  66.9 62.7 all-gather.2

commit v2 on v1

--- a/solution.py
+++ b/solution.py
@@ -15,6 +15,7 @@
 ITEMS = ("x", "z_hi", "y")
 MIB = 1 << 20
 STEP = 256
+FEW = 128
 MOST = 48 * MIB
 HBM = pl.BlockSpec(memory_space=pltpu.HBM)
 FULL = pl.BlockSpec(memory_space=pltpu.VMEM)
@@ -183,33 +184,46 @@
     return fetches
 
 
-def transport_body(target, cols, r, k, came, t_out, other_out, sums_out, picked, sems):
-    rows, codes = k.shape
+def weigh(t_out, other_out, picked, k, r, scale, first):
+    count, codes = t_out.shape
     wide = other_out.shape[1]
-    fetches = fetch_parity(came, picked, 1 - lax.axis_index("core"), sems)
+    r_up = jnp.transpose(jnp.broadcast_to(r[0:1, first : first + count], (8, count)))
+    for i in range(count // FEW):
+        here = slice(i * FEW, (i + 1) * FEW)
+        rows = slice(first + i * FEW, first + (i + 1) * FEW)
+        t_out[here, :] = (r_up[here, 0:1] * k[rows, :].astype(F32) * scale).astype(BF16)
+    yield
+    for i in range(count // FEW):
+        here = slice(i * FEW, (i + 1) * FEW)
+        other_out[here, :] = nt(t_out[here, :], picked[...].reshape(wide, codes)).astype(BF16)
+    yield
+
+
+def transport_body(target, cols, r, k, came, t_out, other_out, sums_out, theirs, ours, sems, our_sems):
+    count = t_out.shape[0]
+    wide = other_out.shape[1]
+    core = lax.axis_index("core")
+    fetches = fetch_parity(came, theirs, 1 - core, sems)
+    our_fetches = fetch_parity(came, ours, core, our_sems)
     scale = target / jnp.sum(cols[...], axis=0)[0:1]
     sums = over_codes(scale, k)
     sums_out[...] = sums
     parts = jnp.concatenate([cut(part.astype(F32), wide) for part in halves(sums)], 0)
     filled = jnp.concatenate([parts, jnp.zeros((16 - parts.shape[0], wide), F32)], 0)
-    other_out[rows : rows + 16, :] = filled.astype(BF16)
-    r_up = jnp.transpose(jnp.broadcast_to(r[0:1, :], (8, r.shape[1])))
+    other_out[count : count + 16, :] = filled.astype(BF16)
+    work = weigh(t_out, other_out, theirs, k, r, scale, 0)
+    next(work)
     for fetch in fetches:
         fetch.wait()
-    for i in range(rows // STEP):
-        here = slice(i * STEP, (i + 1) * STEP)
-        t = (r_up[here, 0:1] * k[here, :].astype(F32) * scale).astype(BF16)
-        t_out[here, :] = t
-        other_out[here, :] = nt(t, picked[...].reshape(wide, codes)).astype(BF16)
-
-
-def mine_body(t, came, out, picked, sems):
-    wide = out.shape[1]
-    for fetch in fetch_parity(came, picked, lax.axis_index("core"), sems):
+    next(work)
+    for fetch in our_fetches:
         fetch.wait()
-    for i in range(t.shape[0] // STEP):
-        here = slice(i * STEP, (i + 1) * STEP)
-        out[here, :] = nt(t[here, :], picked[...].reshape(wide, t.shape[1]))
+
+
+def second_body(target, cols, r, k, theirs, t_out, other_out):
+    scale = target / jnp.sum(cols[...], axis=0)[0:1]
+    for _ in weigh(t_out, other_out, theirs, k, r, scale, k.shape[0] - t_out.shape[0]):
+        pass
 
 
 def pack(sums):
@@ -221,40 +235,67 @@
     return tail[:8] + tail[8:]
 
 
-def pair_body(mine, came, sums, here_out, far_out, sums_out, cross_out, beside_out):
-    rows, wide = mine.shape
+def add_cores(t, ours, came, here_out, far_out, near_out, mine):
+    count, codes = t.shape
+    wide = mine.shape[1]
     width = wide // RING
-    tail = came[rows : rows + 16, :].astype(F32)
-    n = rows // wide
+    for i in range(count // FEW):
+        here = slice(i * FEW, (i + 1) * FEW)
+        mine[here, :] = nt(t[here, :], ours[...].reshape(wide, codes))
+    z = lax.axis_index("z_lo")
+    pair = z + 1 - 2 * (z % 2)
+    far = (z + 2) % RING
+    below = near_out.shape[0] - count
+    for chip, out, at in ((z, here_out, 0), (far, far_out, 0), ((pair + 2) % RING, near_out, 0), (pair, near_out, below)):
+        lanes = pl.ds(pl.multiple_of(chip * width, width), width)
+        value = mine[:, lanes] + came[:count, lanes].astype(F32)
+        out[at : at + count, :] = value.astype(out.dtype)
+
+
+def pair_body(t, ours, came, sums, here_out, far_out, near_out, sums_out, mine):
+    add_cores(t, ours, came, here_out, far_out, near_out, mine)
+    count, wide = mine.shape
+    width = wide // RING
+    tail = came[count : count + 16, :].astype(F32)
+    n = sums.shape[1] // wide
     theirs = [tail[i : i + 1, :] + tail[n + i : n + i + 1, :] for i in range(n)]
     both = cut(sums[...] + jnp.concatenate(theirs, 1), width)
     sums_out[...] = both
-    z = lax.axis_index("z_lo")
-    pair = z + 1 - 2 * (z % 2)
-    far = (z + 2) % RING
-    for chip, out in ((z, here_out), (far, far_out), ((pair + 2) % RING, cross_out), (pair, beside_out)):
-        lanes = pl.ds(pl.multiple_of(chip * width, width), width)
-        value = mine[:, lanes] + came[:rows, lanes].astype(F32)
-        out[:rows, :] = value.astype(out.dtype)
-    cross_out[rows : rows + 16, :] = pack(both)
+    near_out[count : count + 16, :] = pack(both)
+
+
+def second_pair_body(t, ours, came, after, here_out, far_out, near_out, mine):
+    add_cores(t, ours, came, here_out, far_out, near_out, mine)
 
 
 def cross_body(far, came, sums, out, sums_out):
-    rows = far.shape[0]
-    out[:rows, :] = (far[...] + came[:rows, :].astype(F32)).astype(BF16)
-    both = sums[...] + unpack(came[rows : rows + 16, :])
+    count = far.shape[0]
+    out[:count, :] = (far[...] + came[:count, :].astype(F32)).astype(BF16)
+    both = sums[...] + unpack(came[count : count + 16, :])
     sums_out[...] = both
-    out[rows : rows + 16, :] = pack(both)
-
-
-def last_body(own, beside, far, sums, r, out):
+    out[count : count + 16, :] = pack(both)
+
+
+def second_cross_body(far, came, after, out):
+    count = far.shape[0]
+    out[...] = (far[...] + came[:count, :].astype(F32)).astype(BF16)
+
+
+def last_body(own, second_own, near, second_near, far, second_far, sums, r, out):
     rows, width = out.shape
-    total = sums[...] + unpack(far[rows : rows + 16, :])
+    count = own.shape[0]
+    total = sums[...] + unpack(far[count : count + 16, :])
     ratio = jnp.transpose(1.0 / (cut(r[0:1, :], width) * total))
     for i in range(rows // width):
-        here = slice(i * width, (i + 1) * width)
-        value = own[here, :] + beside[here, :].astype(F32) + far[here, :].astype(F32)
-        out[here, :] = (value * ratio[:, i : i + 1]).astype(out.dtype)
+        at = i * width
+        mine, beside, passed = own, near, far
+        if at >= count:
+            at -= count
+            mine, beside, passed = second_own, second_near, second_far
+        below = at + beside.shape[0] - mine.shape[0]
+        value = mine[at : at + width, :] + beside[below : below + width, :].astype(F32)
+        value = value + passed[at : at + width, :].astype(F32)
+        out[i * width : (i + 1) * width, :] = (value * ratio[:, i : i + 1]).astype(out.dtype)
 
 
 def shards(block_two, block_one, codebook_two, codebook_one):
@@ -289,7 +330,7 @@
         "kernel_two",
         [(came_two, HBM), (block_two, HBM)],
         flops=book_flops,
-        limit=MOST,
+        limit=MOST + 4 * MIB - MIB // 4,
         scratch=book_room + [sem((plane + steps,))],
     )
 
@@ -342,42 +383,80 @@
 
     wide = features // 2
     width = features // groups
-    picked = pltpu.VMEM((RING, 2, RING, run, codes), BF16)
-    t, other, sums = call(
+    more_rows = rows // 2
+    few_rows = rows - more_rows
+    parity = (RING, 2, RING, run, codes)
+    t, other, sums, theirs, ours = call(
         functools.partial(transport_body, target),
-        (shape(rows, codes, of=BF16), shape(rows + 16, wide, of=BF16), shape(1, rows)),
+        (
+            shape(more_rows, codes, of=BF16),
+            shape(more_rows + 16, wide, of=BF16),
+            shape(1, rows),
+            shape(*parity, of=BF16),
+            shape(*parity, of=BF16),
+        ),
         "transport",
         [cols, scale, k_two, (came_two, HBM)],
-        flops=book_flops // 2,
-        limit=MOST - 4 * MIB,
-        scratch=[picked, sem((plane,))],
-    )
-    came = lax.ppermute(other, "core", [(0, 1), (1, 0)])
-    mine = call(
-        mine_body,
-        shape(rows, wide),
-        "mine",
-        [t, (came_two, HBM)],
-        flops=book_flops // 2,
-        limit=MOST - 4 * MIB,
-        scratch=[picked, sem((plane,))],
-    )
-    tall = shape(rows + 16, width, of=BF16)
-    own, far, sums, cross, beside = call(
+        flops=2 * more_rows * codes * wide,
+        limit=MOST + MIB // 4,
+        scratch=[sem((plane,)), sem((plane,))],
+    )
+    swap = [(0, 1), (1, 0)]
+    came = lax.ppermute(other, "core", swap)
+    second_t, second_other = call(
+        functools.partial(second_body, target),
+        (shape(few_rows, codes, of=BF16), shape(few_rows, wide, of=BF16)),
+        "second_transport",
+        [cols, scale, k_two, theirs],
+        flops=2 * few_rows * codes * wide,
+    )
+    second_came = lax.ppermute(second_other, "core", swap)
+    own, far, nearing, sums = call(
         pair_body,
-        (shape(rows, width), shape(rows, width), shape(8, width), tall, shape(rows, width, of=BF16)),
+        (
+            shape(more_rows, width),
+            shape(more_rows, width),
+            shape(2 * more_rows + 16, width, of=BF16),
+            shape(8, width),
+        ),
         "pair",
-        [mine, came, sums],
-        limit=24 * MIB,
+        [t, ours, came, sums],
+        flops=2 * more_rows * codes * wide,
+        scratch=[pltpu.VMEM((more_rows, wide), F32)],
     )
     neighbours = [(0, 1), (1, 0), (2, 3), (3, 2)]
-    crossed = lax.ppermute(cross, "z_lo", neighbours)
-    passed, sums = call(cross_body, (tall, shape(8, width)), "cross", [far, crossed, sums])
-    passed, beside = lax.optimization_barrier((passed, beside))
-    passed = lax.ppermute(passed, "z_lo", [(0, 2), (2, 0), (1, 3), (3, 1)])
-    beside = lax.ppermute(beside, "z_lo", neighbours)
+    across = [(0, 2), (2, 0), (1, 3), (3, 1)]
+    near = lax.ppermute(nearing, "z_lo", neighbours)
+    second_own, second_far, second_near = call(
+        second_pair_body,
+        (shape(few_rows, width), shape(few_rows, width), shape(2 * few_rows, width, of=BF16)),
+        "second_pair",
+        [second_t, ours, second_came, (nearing, HBM)],
+        flops=2 * few_rows * codes * wide,
+        scratch=[pltpu.VMEM((few_rows, wide), F32)],
+    )
+    second_near = lax.ppermute(second_near, "z_lo", neighbours)
+    passing, sums = call(
+        cross_body,
+        (shape(more_rows + 16, width, of=BF16), shape(8, width)),
+        "cross",
+        [far, near, sums],
+    )
+    passed = lax.ppermute(passing, "z_lo", across)
+    second_passed = call(
+        second_cross_body,
+        shape(few_rows, width, of=BF16),
+        "second_cross",
+        [second_far, second_near, (passing, HBM)],
+        flops=book_flops,
+        nbytes=32 * MIB,
+    )
+    second_passed = lax.ppermute(second_passed, "z_lo", across)
     rebuilt = call(
-        last_body, shape(rows, width, of=BF16), "last", [own, beside, passed, sums, scale]
+        last_body,
+        shape(rows, width, of=BF16),
+        "last",
+        [own, second_own, near, second_near, passed, second_passed, sums, scale],
     )
     cols_one = jnp.sum(cols[:, 1], axis=0)
     next_log_scale = math.log(target) - jnp.log(cols_one)

time: 246 us -> 245 us (level)
  waiting for transfers between devices: 22.4 us -> 17.1 us
  starting transfers between devices: 16.2 us -> 20.3 us
  Pallas kernels: 23.3 us -> 26.6 us
  local copies, waits for them, and re-layouts: 5.14 us -> 1.96 us
    ppermute x4 -> x6, waiting for transfers between devices: 18.4 us -> 13.1 us  [the longest x1 7.23 us: shards(): second_passed = lax.ppermute(second_passed, 'z_lo', across)]
    ppermute x4 -> x6, starting transfers between devices: 12.9 us -> 17 us  [the longest x1 5.61 us: shards(): came = lax.ppermute(other, 'core', swap)]
    pallas_call x13 -> x15, Pallas kernels: 23.3 us -> 26.6 us  [call(): pl.pallas_call(body, out_shape=outs, in_specs=[spec for _, spec in ins],...]
    unnamed x8 -> x4, local copies, waits for them, and re-layouts: 4.49 us -> 1.31 us
  transfers between devices with their start and end apart: 6 -> 8, of which waited for: 5 -> 4; matrix products, arithmetic and copies ran while one was open for 1% -> 1% of each run, Pallas kernels for 7% -> 8%
where the time goes in v2:
time: 245 us; the launch traced here: 244 us
  blocking collectives  162 us (66%)
  Pallas kernels  26.6 us (11%)
  starting transfers between devices  20.3 us (8%)
  waiting for transfers between devices  17.1 us (7%)
  between operations  14.2 us (6%)
    all_to_all x3, blocking collectives, shards(): gathered = lax.all_to_all(row_sums, CODES, 0, 0)  43.6 us
    all_to_all x2, blocking collectives, shards(): cols = lax.all_to_all(col, 'z_hi', 0, 0)  32.2 us
    all_to_all x1, blocking collectives, shards(): column = lax.all_to_all(both_books, 'z_hi', 0, 0)  29.6 us
    all_to_all x3, blocking collectives, shards(): col = spread(jnp.sum(lax.all_to_all(col, PLANE, 0, 0), axis=0), RING)  28.7 us
    all_to_all x1, blocking collectives, shards(): came_two = lax.all_to_all(two, PLANE, 0, 0)  28.3 us
    pallas_call x15, Pallas kernels, call(): pl.pallas_call(body, out_shape=outs, in_specs=[spec for _, spec in ins],...  26.6 us
    ppermute x1, waiting for transfers between devices, shards(): second_passed = lax.ppermute(second_passed, 'z_lo', across)  7.23 us
    ppermute x1, starting transfers between devices, shards(): came = lax.ppermute(other, 'core', swap)  5.61 us
  transfers between devices with their start and end apart: 8, of which 4 were waited for; matrix products, arithmetic and copies ran while one was open for 1% of the time, Pallas kernels for 8%

profile of v2, /device:TPU:1, one launch (start us, length us, event | category | flops | bytes accessed | tf_op | source)
XLA Modules:
  0.0 244.3 jit_solution(8684189362925066019)
XLA Ops:
  8.0 29.6 %all_to_all.55.column = bf16[4,32,1024]{2,1,0:T(8,128)(2,1)S(1)} all-to-all(bf16[4,32,1024]{2,1,0:T(8,128)(2,1)S(1)} %broadcast_in_dim.8), channel_id=1, replica_groups=mesh['x'=4,'z_hi'=4,'y'=4,'z_lo'=4,'core'=2] {'z_hi'}, dimensions={0} | all-to-all | bytes 524288 | tf_op jit(solution)/shard_map/all_to_all | solution.py:313
  38.4 28.3 %all_to_all.56.came = bf16[16,4,16,1024]{3,2,1,0:T(8,128)(2,1)} all-to-all(bf16[16,4,16,1024]{3,2,1,0:T(8,128)(2,1)S(1)} %get-tuple-element.30), channel_id=1, replica_groups=mesh['x'=4,'z_hi'=4,'y'=4,'z_lo'=4,'core'=2] {'x','y'}, dimensions={0} | all-to-all | bytes 4194304 | tf_op jit(solution)/shard_map/all_to_all | solution.py:320
  66.7 5.9 %kernel_two.1 = (bf16[1024,1024]{1,0:T(8,128)(2,1)S(1)}, f32[8,1,1024]{2,1,0:T(1,128)S(1)}) custom-call(bf16[16,4,16,1024]{3,2,1,0:T(8,128)(2,1)} %all_to_all.56.came, bf16[1024,1024]{1,0:T(8,128)(2,1)} %block.2), custom_call_target="tpu_custom_call" | custom-call | flops 2147483648 | bytes 4194304 | tf_op jit(solution)/shard_map/kernel_two/pallas_call | solution.py:29
  72.6 21.8 %all_to_all.57.gathered = f32[8,1,1024]{2,1,0:T(1,128)S(1)} all-to-all(f32[8,1,1024]{2,1,0:T(1,128)S(1)} %get-tuple-element.33), channel_id=1, replica_groups=mesh['x'=4,'z_hi'=4,'y'=4,'z_lo'=4,'core'=2] {'z_lo','core'}, dimensions={0} | all-to-all | bytes 65536 | tf_op jit(solution)/shard_map/all_to_all | solution.py:354
  95.3 9.5 %all_to_all.58 = f32[16,1,1024]{2,1,0:T(1,128)S(1)} all-to-all(f32[16,1,1024]{2,1,0:T(1,128)S(1)} %get-tuple-element.35), channel_id=1, replica_groups=mesh['x'=4,'z_hi'=4,'y'=4,'z_lo'=4,'core'=2] {'x','y'}, dimensions={0} | all-to-all | bytes 131072 | tf_op jit(solution)/shard_map/all_to_all | solution.py:370
  104.8 14.4 %all_to_all.59.cols = f32[4,1,1024]{2,1,0:T(1,128)S(1)} all-to-all(f32[4,1,1024]{2,1,0:T(1,128)S(1)} %broadcast_in_dim.9), channel_id=1, replica_groups=mesh['x'=4,'z_hi'=4,'y'=4,'z_lo'=4,'core'=2] {'z_hi'}, dimensions={0} | all-to-all | bytes 32768 | tf_op jit(solution)/shard_map/all_to_all | solution.py:371
  119.9 11.1 %all_to_all.60.gathered = f32[8,1,1024]{2,1,0:T(1,128)S(1)} all-to-all(f32[8,1,1024]{2,1,0:T(1,128)S(1)} %rows.2), channel_id=1, replica_groups=mesh['x'=4,'z_hi'=4,'y'=4,'z_lo'=4,'core'=2] {'z_lo','core'}, dimensions={0} | all-to-all | bytes 65536 | tf_op jit(solution)/shard_map/all_to_all | solution.py:354
  131.8 9.6 %all_to_all.61 = f32[16,1,1024]{2,1,0:T(1,128)S(1)} all-to-all(f32[16,1,1024]{2,1,0:T(1,128)S(1)} %get-tuple-element.36), channel_id=1, replica_groups=mesh['x'=4,'z_hi'=4,'y'=4,'z_lo'=4,'core'=2] {'x','y'}, dimensions={0} | all-to-all | bytes 131072 | tf_op jit(solution)/shard_map/all_to_all | solution.py:370
  142.1 3.2 %all-to-all-start.7 = ((f32[4,1,1024]{2,1,0:T(1,128)}), f32[4,1,1024]{2,1,0:T(1,128)S(1)}, u32[]{:S(2)}, u32[]{:S(2)}) async-start(f32[4,1,1024]{2,1,0:T(1,128)} %broadcast_in_dim.10.after), calls=%async_computation.7 | async-start | bytes 32768 | tf_op jit(solution)/shard_map/all_to_all | solution.py:371
  145.4 6.0 %kernel_one.1 = (bf16[1024,1024]{1,0:T(8,128)(2,1)S(1)}, f32[8,1,1024]{2,1,0:T(1,128)S(1)}) custom-call(bf16[16,4,16,1024]{3,2,1,0:T(8,128)(2,1)} %bitcast.5, bf16[1024,1024]{1,0:T(8,128)(2,1)} %block.3, f32[4,1,1024]{2,1,0:T(1,128)} %broadcast_in_dim.10.after), custom_call_target="tpu_custom_call" | custom-call | flops 2147483648 | bytes 4194304 | tf_op jit(solution)/shard_map/kernel_one/pallas_call | solution.py:29
  152.7 4.0 %all-to-all-done.7.cols = f32[4,1,1024]{2,1,0:T(1,128)S(1)} async-done(((f32[4,1,1024]{2,1,0:T(1,128)}), f32[4,1,1024]{2,1,0:T(1,128)S(1)}, u32[]{:S(2)}, u32[]{:S(2)}) %all-to-all-start.7) | async-done | bytes 16416 | tf_op jit(solution)/shard_map/all_to_all | solution.py:371
  157.4 10.8 %all_to_all.62.gathered = f32[8,2,1024]{2,1,0:T(2,128)S(1)} all-to-all(f32[8,2,1024]{2,1,0:T(2,128)S(1)} %rows.3), channel_id=1, replica_groups=mesh['x'=4,'z_hi'=4,'y'=4,'z_lo'=4,'core'=2] {'z_lo','core'}, dimensions={0} | all-to-all | bytes 131072 | tf_op jit(solution)/shard_map/all_to_all | solution.py:354
  169.2 9.6 %all_to_all.63 = f32[16,2,1024]{2,1,0:T(2,128)S(1)} all-to-all(f32[16,2,1024]{2,1,0:T(2,128)S(1)} %get-tuple-element.40), channel_id=1, replica_groups=mesh['x'=4,'z_hi'=4,'y'=4,'z_lo'=4,'core'=2] {'x','y'}, dimensions={0} | all-to-all | bytes 262144 | tf_op jit(solution)/shard_map/all_to_all | solution.py:370
  178.9 17.8 %all_to_all.64.cols = f32[4,2,1024]{2,1,0:T(2,128)S(1)} all-to-all(f32[4,2,1024]{2,1,0:T(2,128)S(1)} %broadcast_in_dim.11), channel_id=1, replica_groups=mesh['x'=4,'z_hi'=4,'y'=4,'z_lo'=4,'core'=2] {'z_hi'}, dimensions={0} | all-to-all | bytes 65536 | tf_op jit(solution)/shard_map/all_to_all | solution.py:371
  196.7 3.7 %transport.1 = (bf16[512,1024]{1,0:T(8,128)(2,1)S(1)}, bf16[528,512]{1,0:T(8,128)(2,1)S(1)}, f32[1,1024]{1,0:T(1,128)S(1)}, bf16[4,2,4,16,1024]{4,3,2,1,0:T(8,128)(2,1)S(1)}, bf16[4,2,4,16,1024]{4,3,2,1,0:T(8,128)(2,1)S(1)}) custom-call(f32[4,2,1024]{2,1,0:T(2,128)S(1)} %all_to_all.64.cols, f32[1,1024]{1,0:T(1,128)S(1)} %get-tuple-element.41.r, ...), custom_call_target="tpu_custom_call" | custom-call | flops 536870912 | bytes 4194304 | tf_op jit(solution)/shard_map/transport/pallas_call | solution.py:29
  200.4 5.6 %collective-permute-start = (bf16[528,512]{1,0:T(8,128)(2,1)S(1)}, bf16[528,512]{1,0:T(8,128)(2,1)S(1)}, u32[]{:S(2)}, u32[]{:S(2)}) collective-permute-start(bf16[528,512]{1,0:T(8,128)(2,1)S(1)} %get-tuple-element.44), channel_id=1, source_target_pairs={{0,1},{1,0},{2,3},{3,2},{4,5},{5,4},{6,7},{7,6},{8,9},{9,8},{10,11... | collective-permute-start | bytes 1622024 | tf_op jit(solution)/shard_map/ppermute | solution.py:405
  207.8 1.9 collective-permute-start.1
  211.4 2.4 collective-permute-start.2
  215.5 2.9 %collective-permute-start.3 = (bf16[1024,128]{1,0:T(8,128)(2,1)S(1)}, bf16[1024,128]{1,0:T(8,128)(2,1)S(1)}, u32[]{:S(2)}, u32[]{:S(2)}) collective-permute-start(bf16[1024,128]{1,0:T(8,128)(2,1)S(1)} %get-tuple-element.52), channel_id=1, source_target_pairs={{0,2},{2,0},{4,6},{6,4},{1,3},{3,1},{5,7},{7,5},{8,10},{10,8},{12,... | collective-permute-start | bytes 786440 | tf_op jit(solution)/shard_map/ppermute | solution.py:438
  218.4 2.3 collective-permute-done.2.came.near
  220.8 2.1 collective-permute-start.4
  222.9 3.5 %collective-permute-done.3.came.second_near = bf16[1024,128]{1,0:T(8,128)(2,1)S(1)} collective-permute-done((bf16[1024,128]{1,0:T(8,128)(2,1)S(1)}, bf16[1024,128]{1,0:T(8,128)(2,1)S(1)}, u32[]{:S(2)}, u32[]{:S(2)}) %collective-permute-start.3) | collective-permute-done | bytes 262176 | tf_op jit(solution)/shard_map/ppermute | solution.py:438
  226.4 2.1 collective-permute-start.5
  229.1 7.2 %collective-permute-done.5.second_far = bf16[512,128]{1,0:T(8,128)(2,1)S(1)} collective-permute-done((bf16[512,128]{1,0:T(8,128)(2,1)S(1)}, bf16[512,128]{1,0:T(8,128)(2,1)S(1)}, u32[]{:S(2)}, u32[]{:S(2)}) %collective-permute-start.5) | collective-permute-done | bytes 131104 | tf_op jit(solution)/shard_map/ppermute | solution.py:454
  (32 shorter events, 14.6 us)
Async XLA Ops:
  7.2 138.2 %all-gather.3.cloned.1.call-start = ((), (), s32[]{:S(2)}) async-start(), calls=%async_computation.11 | async-start | bytes 2228224 | tf_op jit(solution)/shard_map/all_gather | solution.py:322
  142.1 14.7 %all-to-all-start.7 = ((f32[4,1,1024]{2,1,0:T(1,128)}), f32[4,1,1024]{2,1,0:T(1,128)S(1)}, u32[]{:S(2)}, u32[]{:S(2)}) async-start(f32[4,1,1024]{2,1,0:T(1,128)} %broadcast_in_dim.10.after), calls=%async_computation.7 | async-start | bytes 32768 | tf_op jit(solution)/shard_map/all_to_all | solution.py:371
  151.4 1.3 copy-start
  156.7 11.5 %copy-start.1 = (bf16[1024,1024]{1,0:T(8,128)(2,1)S(1)}, bf16[1024,1024]{1,0:T(8,128)(2,1)}, u32[]{:S(2)}) copy-start(bf16[1024,1024]{1,0:T(8,128)(2,1)} %copy-done) | copy-start | bytes 6291460
  200.4 9.3 %collective-permute-start = (bf16[528,512]{1,0:T(8,128)(2,1)S(1)}, bf16[528,512]{1,0:T(8,128)(2,1)S(1)}, u32[]{:S(2)}, u32[]{:S(2)}) collective-permute-start(bf16[528,512]{1,0:T(8,128)(2,1)S(1)} %get-tuple-element.44), channel_id=1, source_target_pairs={{0,1},{1,0},{2,3},{3,2},{4,5},{5,4},{6,7},{7,6},{8,9},{9,8},{10,11... | collective-permute-start | bytes 1622024 | tf_op jit(solution)/shard_map/ppermute | solution.py:405
  207.8 6.0 %collective-permute-start.1 = (bf16[512,512]{1,0:T(8,128)(2,1)S(1)}, bf16[512,512]{1,0:T(8,128)(2,1)S(1)}, u32[]{:S(2)}, u32[]{:S(2)}) collective-permute-start(bf16[512,512]{1,0:T(8,128)(2,1)S(1)} %get-tuple-element.49), channel_id=1, source_target_pairs={{0,1},{1,0},{2,3},{3,2},{4,5},{5,4},{6,7},{7,6},{8,9},{9,8},{10,11... | collective-permute-start | bytes 1572872 | tf_op jit(solution)/shard_map/ppermute | solution.py:413
  211.4 9.4 %collective-permute-start.2 = (bf16[1040,128]{1,0:T(8,128)(2,1)S(1)}, bf16[1040,128]{1,0:T(8,128)(2,1)S(1)}, u32[]{:S(2)}, u32[]{:S(2)}) collective-permute-start(bf16[1040,128]{1,0:T(8,128)(2,1)S(1)} %get-tuple-element.50.after), channel_id=1, source_target_pairs={{0,2},{2,0},{4,6},{6,4},{1,3},{3,1},{5,7},{7,5},{8,10},{10,8},{12,... | collective-permute-start | bytes 798728 | tf_op jit(solution)/shard_map/ppermute | solution.py:429
  215.5 10.9 %collective-permute-start.3 = (bf16[1024,128]{1,0:T(8,128)(2,1)S(1)}, bf16[1024,128]{1,0:T(8,128)(2,1)S(1)}, u32[]{:S(2)}, u32[]{:S(2)}) collective-permute-start(bf16[1024,128]{1,0:T(8,128)(2,1)S(1)} %get-tuple-element.52), channel_id=1, source_target_pairs={{0,2},{2,0},{4,6},{6,4},{1,3},{3,1},{5,7},{7,5},{8,10},{10,8},{12,... | collective-permute-start | bytes 786440 | tf_op jit(solution)/shard_map/ppermute | solution.py:438
  220.8 15.6 %collective-permute-start.4 = (bf16[528,128]{1,0:T(8,128)(2,1)S(1)}, bf16[528,128]{1,0:T(8,128)(2,1)S(1)}, u32[]{:S(2)}, u32[]{:S(2)}) collective-permute-start(bf16[528,128]{1,0:T(8,128)(2,1)S(1)} %get-tuple-element.55.after), channel_id=1, source_target_pairs={{0,4},{4,0},{2,6},{6,2},{1,5},{5,1},{3,7},{7,3},{8,12},{12,8},{10,... | collective-permute-start | bytes 405512 | tf_op jit(solution)/shard_map/ppermute | solution.py:445
  226.4 9.9 %collective-permute-start.5 = (bf16[512,128]{1,0:T(8,128)(2,1)S(1)}, bf16[512,128]{1,0:T(8,128)(2,1)S(1)}, u32[]{:S(2)}, u32[]{:S(2)}) collective-permute-start(bf16[512,128]{1,0:T(8,128)(2,1)S(1)} %second_cross.1), channel_id=1, source_target_pairs={{0,4},{4,0},{2,6},{6,2},{1,5},{5,1},{3,7},{7,3},{8,12},{12,8},{10,... | collective-permute-start | bytes 393224 | tf_op jit(solution)/shard_map/ppermute | solution.py:454
Sparse Core Ops, SparseCore 0:
  66.9 62.7 all-gather.2

commit v3 on v1

--- a/solution.py
+++ b/solution.py
@@ -155,7 +155,7 @@
     col_out[:, 1:2, :] = spread(over_items(scale[1:2], held), copies)
 
 
-def row_body(target, groups, cols, k, *refs):
+def row_body(target, groups, cols, k, after, *refs):
     out = refs[-1]
     scale = target / jnp.sum(cols[...], axis=0)[0:1]
     out[:, 0:1, :] = spread(over_codes(scale, k), groups)
@@ -172,21 +172,24 @@
     return jnp.concatenate([row[:, i : i + width] for i in range(0, row.shape[1], width)], 0)
 
 
-def fetch_parity(came, picked, parity, sems):
-    fetches = []
-    for x in range(RING):
-        for y in range(RING):
-            here = came.at[x * RING + y, pl.ds(2 * parity, 2)]
-            move = pltpu.make_async_copy(here, picked.at[x, :, y], sems.at[x * RING + y])
-            move.start()
-            fetches.append(move)
-    return fetches
-
-
-def transport_body(target, cols, r, k, came, t_out, other_out, sums_out, picked, sems):
-    rows, codes = k.shape
+def turn_body(groups, came, after, out, book, sems):
+    features, codes = out.shape[1], out.shape[0]
+    for fetch in fetch_book(came, book, sems):
+        fetch.wait()
+    width = features // groups
+    core = lax.axis_index("core")
+    z_hi = width // (RING * book.shape[3])
+    for mine in range(2):
+        parity = core if mine else 1 - core
+        for x in range(RING):
+            to = (mine * RING + x) * width
+            part = book[x, pl.ds(z_hi * parity, z_hi)].reshape(width, codes)
+            out[:, to : to + width] = part.T
+
+
+def transport_body(target, cols, r, k, turned, t_out, other_out, sums_out):
+    rows = k.shape[0]
     wide = other_out.shape[1]
-    fetches = fetch_parity(came, picked, 1 - lax.axis_index("core"), sems)
     scale = target / jnp.sum(cols[...], axis=0)[0:1]
     sums = over_codes(scale, k)
     sums_out[...] = sums
@@ -194,22 +197,18 @@
     filled = jnp.concatenate([parts, jnp.zeros((16 - parts.shape[0], wide), F32)], 0)
     other_out[rows : rows + 16, :] = filled.astype(BF16)
     r_up = jnp.transpose(jnp.broadcast_to(r[0:1, :], (8, r.shape[1])))
-    for fetch in fetches:
-        fetch.wait()
     for i in range(rows // STEP):
         here = slice(i * STEP, (i + 1) * STEP)
         t = (r_up[here, 0:1] * k[here, :].astype(F32) * scale).astype(BF16)
         t_out[here, :] = t
-        other_out[here, :] = nt(t, picked[...].reshape(wide, codes)).astype(BF16)
-
-
-def mine_body(t, came, out, picked, sems):
+        other_out[here, :] = nn(t, turned[:, :wide]).astype(BF16)
+
+
+def mine_body(t, turned, out):
     wide = out.shape[1]
-    for fetch in fetch_parity(came, picked, lax.axis_index("core"), sems):
-        fetch.wait()
     for i in range(t.shape[0] // STEP):
         here = slice(i * STEP, (i + 1) * STEP)
-        out[here, :] = nt(t[here, :], picked[...].reshape(wide, t.shape[1]))
+        out[here, :] = nn(t[here, :], turned[:, wide:])
 
 
 def pack(sums):
@@ -289,7 +288,7 @@
         "kernel_two",
         [(came_two, HBM), (block_two, HBM)],
         flops=book_flops,
-        limit=MOST,
+        limit=MOST + 4 * MIB - MIB // 4,
         scratch=book_room + [sem((plane + steps,))],
     )
 
@@ -300,12 +299,12 @@
             "kernel_one",
             [(came_one, HBM), (block_one, HBM), (after, HBM)],
             flops=book_flops,
-            limit=MOST + 2 * MIB,
+            limit=MOST + 4 * MIB - MIB // 4,
             scratch=book_room + [pltpu.VMEM((rows, codes), BF16), sem((plane + steps,)), sem((steps,))],
             out_specs=(HBM, FULL),
         )
 
-    more = []
+    more, turned = [], k_two
     small = 32 * rows * codes
     for sweep in range(SWEEPS):
         last = sweep == SWEEPS - 1
@@ -330,37 +329,37 @@
         cols = lax.all_to_all(col, "z_hi", 0, 0)
         if sweep == 1:
             k_one, first_one = make_k_one(col)
+            turned = call(
+                functools.partial(turn_body, groups),
+                shape(codes, features, of=BF16),
+                "turn",
+                [(came_two, HBM), (first_one, HBM)],
+                limit=MOST + 2 * MIB,
+                scratch=[book_room[0], sem((plane,))],
+            )
             more = [first_one]
         if not last:
             row_sums = call(
                 functools.partial(row_body, target, groups),
                 shape(groups, 1 + len(more), rows),
                 "rows",
-                [cols, k_two] + more,
+                [cols, k_two, (turned, HBM)] + more,
                 flops=small,
             )
 
     wide = features // 2
     width = features // groups
-    picked = pltpu.VMEM((RING, 2, RING, run, codes), BF16)
     t, other, sums = call(
         functools.partial(transport_body, target),
         (shape(rows, codes, of=BF16), shape(rows + 16, wide, of=BF16), shape(1, rows)),
         "transport",
-        [cols, scale, k_two, (came_two, HBM)],
+        [cols, scale, k_two, turned],
         flops=book_flops // 2,
-        limit=MOST - 4 * MIB,
-        scratch=[picked, sem((plane,))],
+        limit=24 * MIB,
     )
     came = lax.ppermute(other, "core", [(0, 1), (1, 0)])
     mine = call(
-        mine_body,
-        shape(rows, wide),
-        "mine",
-        [t, (came_two, HBM)],
-        flops=book_flops // 2,
-        limit=MOST - 4 * MIB,
-        scratch=[picked, sem((plane,))],
+        mine_body, shape(rows, wide), "mine", [t, turned], flops=book_flops // 2, limit=24 * MIB
     )
     tall = shape(rows + 16, width, of=BF16)
     own, far, sums, cross, beside = call(
@@ -372,10 +371,9 @@
     )
     neighbours = [(0, 1), (1, 0), (2, 3), (3, 2)]
     crossed = lax.ppermute(cross, "z_lo", neighbours)
+    beside = lax.ppermute(beside, "z_lo", neighbours)
     passed, sums = call(cross_body, (tall, shape(8, width)), "cross", [far, crossed, sums])
-    passed, beside = lax.optimization_barrier((passed, beside))
     passed = lax.ppermute(passed, "z_lo", [(0, 2), (2, 0), (1, 3), (3, 1)])
-    beside = lax.ppermute(beside, "z_lo", neighbours)
     rebuilt = call(
         last_body, shape(rows, width, of=BF16), "last", [own, beside, passed, sums, scale]
     )

time: 246 us -> 248 us (level)
  blocking collectives: 162 us -> 166 us
  waiting for transfers between devices: 22.4 us -> 18.8 us
    ppermute x1, waiting for transfers between devices: 4.4 us -> 10.4 us  [shards(): passed = lax.ppermute(passed, 'z_lo', [(0, 2), (2, 0), (1, 3), (3, 1)])]
    ppermute x1, waiting for transfers between devices: 6.73 us -> 2.81 us  [shards(): beside = lax.ppermute(beside, 'z_lo', neighbours)]
    all_to_all x1, waiting for transfers between devices: 4.01 us -> 0.26 us  [shards(): cols = lax.all_to_all(col, 'z_hi', 0, 0)]
    all_to_all x2, blocking collectives: 32.4 us -> 36 us  [shards(): cols = lax.all_to_all(col, 'z_hi', 0, 0)]
    ppermute x1, waiting for transfers between devices: 7.13 us -> 4.2 us  [shards(): crossed = lax.ppermute(cross, 'z_lo', neighbours)]
    unnamed x8 -> x10, local copies, waits for them, and re-layouts: 4.49 us -> 5.82 us
    pallas_call x13 -> x14, Pallas kernels: 23.3 us -> 23.8 us  [call(): pl.pallas_call(body, out_shape=outs, in_specs=[spec for _, spec in ins],...]
where the time goes in v3:
time: 248 us; the launch traced here: 247 us
  blocking collectives  166 us (67%)
  Pallas kernels  23.8 us (10%)
  waiting for transfers between devices  18.8 us (8%)
  starting transfers between devices  16.3 us (7%)
  between operations  14.2 us (6%)
  local copies, waits for them, and re-layouts  6.47 us (3%)
    all_to_all x3, blocking collectives, shards(): gathered = lax.all_to_all(row_sums, CODES, 0, 0)  43.6 us
    all_to_all x2, blocking collectives, shards(): cols = lax.all_to_all(col, 'z_hi', 0, 0)  36 us
    all_to_all x1, blocking collectives, shards(): column = lax.all_to_all(both_books, 'z_hi', 0, 0)  29.6 us
    all_to_all x3, blocking collectives, shards(): col = spread(jnp.sum(lax.all_to_all(col, PLANE, 0, 0), axis=0), RING)  28.7 us
    all_to_all x1, blocking collectives, shards(): came_two = lax.all_to_all(two, PLANE, 0, 0)  28.3 us
    pallas_call x14, Pallas kernels, call(): pl.pallas_call(body, out_shape=outs, in_specs=[spec for _, spec in ins],...  23.8 us
    ppermute x1, waiting for transfers between devices, shards(): passed = lax.ppermute(passed, 'z_lo', [(0, 2), (2, 0), (1, 3), (3, 1)])  10.4 us
    unnamed x10, local copies, waits for them, and re-layouts  5.82 us
  transfers between devices with their start and end apart: 6, of which 5 were waited for; matrix products, arithmetic and copies ran while one was open for 1% of the time, Pallas kernels for 7%

profile of v3, /device:TPU:1, one launch (start us, length us, event | category | flops | bytes accessed | tf_op | source)
XLA Modules:
  0.0 247.3 jit_solution(6756492329994985215)
XLA Ops:
  8.0 29.6 %all_to_all.55.column = bf16[4,32,1024]{2,1,0:T(8,128)(2,1)S(1)} all-to-all(bf16[4,32,1024]{2,1,0:T(8,128)(2,1)S(1)} %broadcast_in_dim.8), channel_id=1, replica_groups=mesh['x'=4,'z_hi'=4,'y'=4,'z_lo'=4,'core'=2] {'z_hi'}, dimensions={0} | all-to-all | bytes 524288 | tf_op jit(solution)/shard_map/all_to_all | solution.py:271
  38.4 28.3 %all_to_all.56.came = bf16[16,4,16,1024]{3,2,1,0:T(8,128)(2,1)} all-to-all(bf16[16,4,16,1024]{3,2,1,0:T(8,128)(2,1)S(1)} %get-tuple-element.24), channel_id=1, replica_groups=mesh['x'=4,'z_hi'=4,'y'=4,'z_lo'=4,'core'=2] {'x','y'}, dimensions={0} | all-to-all | bytes 4194304 | tf_op jit(solution)/shard_map/all_to_all | solution.py:278
  66.7 5.9 %kernel_two.1 = (bf16[1024,1024]{1,0:T(8,128)(2,1)S(1)}, f32[8,1,1024]{2,1,0:T(1,128)S(1)}) custom-call(bf16[16,4,16,1024]{3,2,1,0:T(8,128)(2,1)} %all_to_all.56.came, bf16[1024,1024]{1,0:T(8,128)(2,1)} %block.2), custom_call_target="tpu_custom_call" | custom-call | flops 2147483648 | bytes 4194304 | tf_op jit(solution)/shard_map/kernel_two/pallas_call | solution.py:28
  72.6 21.8 %all_to_all.57.gathered = f32[8,1,1024]{2,1,0:T(1,128)S(1)} all-to-all(f32[8,1,1024]{2,1,0:T(1,128)S(1)} %get-tuple-element.27), channel_id=1, replica_groups=mesh['x'=4,'z_hi'=4,'y'=4,'z_lo'=4,'core'=2] {'z_lo','core'}, dimensions={0} | all-to-all | bytes 65536 | tf_op jit(solution)/shard_map/all_to_all | solution.py:312
  95.3 9.5 %all_to_all.58 = f32[16,1,1024]{2,1,0:T(1,128)S(1)} all-to-all(f32[16,1,1024]{2,1,0:T(1,128)S(1)} %get-tuple-element.29), channel_id=1, replica_groups=mesh['x'=4,'z_hi'=4,'y'=4,'z_lo'=4,'core'=2] {'x','y'}, dimensions={0} | all-to-all | bytes 131072 | tf_op jit(solution)/shard_map/all_to_all | solution.py:328
  104.8 14.4 %all_to_all.59.cols = f32[4,1,1024]{2,1,0:T(1,128)S(1)} all-to-all(f32[4,1,1024]{2,1,0:T(1,128)S(1)} %broadcast_in_dim.9), channel_id=1, replica_groups=mesh['x'=4,'z_hi'=4,'y'=4,'z_lo'=4,'core'=2] {'z_hi'}, dimensions={0} | all-to-all | bytes 32768 | tf_op jit(solution)/shard_map/all_to_all | solution.py:329
  119.9 11.1 %all_to_all.60.gathered = f32[8,1,1024]{2,1,0:T(1,128)S(1)} all-to-all(f32[8,1,1024]{2,1,0:T(1,128)S(1)} %rows.2), channel_id=1, replica_groups=mesh['x'=4,'z_hi'=4,'y'=4,'z_lo'=4,'core'=2] {'z_lo','core'}, dimensions={0} | all-to-all | bytes 65536 | tf_op jit(solution)/shard_map/all_to_all | solution.py:312
  131.8 9.6 %all_to_all.61 = f32[16,1,1024]{2,1,0:T(1,128)S(1)} all-to-all(f32[16,1,1024]{2,1,0:T(1,128)S(1)} %get-tuple-element.30), channel_id=1, replica_groups=mesh['x'=4,'z_hi'=4,'y'=4,'z_lo'=4,'core'=2] {'x','y'}, dimensions={0} | all-to-all | bytes 131072 | tf_op jit(solution)/shard_map/all_to_all | solution.py:328
  142.1 3.2 %all-to-all-start.7 = ((f32[4,1,1024]{2,1,0:T(1,128)}), f32[4,1,1024]{2,1,0:T(1,128)S(1)}, u32[]{:S(2)}, u32[]{:S(2)}) async-start(f32[4,1,1024]{2,1,0:T(1,128)} %broadcast_in_dim.10.after), calls=%async_computation.7 | async-start | bytes 32768 | tf_op jit(solution)/shard_map/all_to_all | solution.py:329
  145.4 6.0 %kernel_one.1 = (bf16[1024,1024]{1,0:T(8,128)(2,1)S(1)}, f32[8,1,1024]{2,1,0:T(1,128)S(1)}) custom-call(bf16[16,4,16,1024]{3,2,1,0:T(8,128)(2,1)} %bitcast.5, bf16[1024,1024]{1,0:T(8,128)(2,1)} %block.3, f32[4,1,1024]{2,1,0:T(1,128)} %broadcast_in_dim.10.after), custom_call_target="tpu_custom_call" | custom-call | flops 2147483648 | bytes 4194304 | tf_op jit(solution)/shard_map/kernel_one/pallas_call | solution.py:28
  152.7 2.4 turn.1.after.turned
  156.7 1.6 copy-done.1
  159.0 10.8 %all_to_all.62.gathered = f32[8,2,1024]{2,1,0:T(2,128)S(1)} all-to-all(f32[8,2,1024]{2,1,0:T(2,128)S(1)} %rows.3), channel_id=1, replica_groups=mesh['x'=4,'z_hi'=4,'y'=4,'z_lo'=4,'core'=2] {'z_lo','core'}, dimensions={0} | all-to-all | bytes 131072 | tf_op jit(solution)/shard_map/all_to_all | solution.py:312
  170.8 9.6 %all_to_all.63 = f32[16,2,1024]{2,1,0:T(2,128)S(1)} all-to-all(f32[16,2,1024]{2,1,0:T(2,128)S(1)} %get-tuple-element.34), channel_id=1, replica_groups=mesh['x'=4,'z_hi'=4,'y'=4,'z_lo'=4,'core'=2] {'x','y'}, dimensions={0} | all-to-all | bytes 262144 | tf_op jit(solution)/shard_map/all_to_all | solution.py:328
  180.5 21.6 %all_to_all.64.cols = f32[4,2,1024]{2,1,0:T(2,128)S(1)} all-to-all(f32[4,2,1024]{2,1,0:T(2,128)S(1)} %broadcast_in_dim.11), channel_id=1, replica_groups=mesh['x'=4,'z_hi'=4,'y'=4,'z_lo'=4,'core'=2] {'z_hi'}, dimensions={0} | all-to-all | bytes 65536 | tf_op jit(solution)/shard_map/all_to_all | solution.py:329
  202.1 1.6 copy-done.2
  203.7 1.9 transport.1
  205.6 5.6 %collective-permute-start = (bf16[1040,512]{1,0:T(8,128)(2,1)S(1)}, bf16[1040,512]{1,0:T(8,128)(2,1)S(1)}, u32[]{:S(2)}, u32[]{:S(2)}) collective-permute-start(bf16[1040,512]{1,0:T(8,128)(2,1)S(1)} %get-tuple-element.37), channel_id=1, source_target_pairs={{0,1},{1,0},{2,3},{3,2},{4,5},{5,4},{6,7},{7,6},{8,9},{9,8},{10,11... | collective-permute-start | bytes 3194888 | tf_op jit(solution)/shard_map/ppermute | solution.py:360
  213.9 2.4 collective-permute-start.2
  216.3 2.9 %collective-permute-start.1 = (bf16[1024,128]{1,0:T(8,128)(2,1)S(1)}, bf16[1024,128]{1,0:T(8,128)(2,1)S(1)}, u32[]{:S(2)}, u32[]{:S(2)}) collective-permute-start(bf16[1024,128]{1,0:T(8,128)(2,1)S(1)} %get-tuple-element.40), channel_id=1, source_target_pairs={{0,2},{2,0},{4,6},{6,4},{1,3},{3,1},{5,7},{7,5},{8,10},{10,8},{12,... | collective-permute-start | bytes 786440 | tf_op jit(solution)/shard_map/ppermute | solution.py:374
  219.2 4.2 %collective-permute-done.2.came = bf16[1040,128]{1,0:T(8,128)(2,1)S(1)} collective-permute-done((bf16[1040,128]{1,0:T(8,128)(2,1)S(1)}, bf16[1040,128]{1,0:T(8,128)(2,1)S(1)}, u32[]{:S(2)}, u32[]{:S(2)}) %collective-permute-start.2) | collective-permute-done | bytes 266272 | tf_op jit(solution)/shard_map/ppermute | solution.py:373
  223.5 2.1 collective-permute-start.3
  226.2 2.8 %collective-permute-done.1.beside = bf16[1024,128]{1,0:T(8,128)(2,1)S(1)} collective-permute-done((bf16[1024,128]{1,0:T(8,128)(2,1)S(1)}, bf16[1024,128]{1,0:T(8,128)(2,1)S(1)}, u32[]{:S(2)}, u32[]{:S(2)}) %collective-permute-start.1) | collective-permute-done | bytes 262176 | tf_op jit(solution)/shard_map/ppermute | solution.py:374
  229.0 10.4 %collective-permute-done.3.far = bf16[1040,128]{1,0:T(8,128)(2,1)S(1)} collective-permute-done((bf16[1040,128]{1,0:T(8,128)(2,1)S(1)}, bf16[1040,128]{1,0:T(8,128)(2,1)S(1)}, u32[]{:S(2)}, u32[]{:S(2)}) %collective-permute-start.3) | collective-permute-done | bytes 266272 | tf_op jit(solution)/shard_map/ppermute | solution.py:376
  (33 shorter events, 13.8 us)
Async XLA Ops:
  7.2 138.2 %all-gather.3.cloned.1.call-start = ((), (), s32[]{:S(2)}) async-start(), calls=%async_computation.11 | async-start | bytes 2228224 | tf_op jit(solution)/shard_map/all_gather | solution.py:280
  142.1 14.7 %all-to-all-start.7 = ((f32[4,1,1024]{2,1,0:T(1,128)}), f32[4,1,1024]{2,1,0:T(1,128)S(1)}, u32[]{:S(2)}, u32[]{:S(2)}) async-start(f32[4,1,1024]{2,1,0:T(1,128)} %broadcast_in_dim.10.after), calls=%async_computation.7 | async-start | bytes 32768 | tf_op jit(solution)/shard_map/all_to_all | solution.py:329
  151.4 1.3 copy-start.3
  155.2 1.3 copy-start
  156.7 1.6 copy-start.1
  158.3 11.5 %copy-start.4 = (bf16[1024,1024]{1,0:T(8,128)(2,1)S(1)}, bf16[1024,1024]{1,0:T(8,128)(2,1)}, u32[]{:S(2)}) copy-start(bf16[1024,1024]{1,0:T(8,128)(2,1)} %copy-done.3) | copy-start | bytes 6291460
  202.1 1.6 copy-start.2
  205.6 7.9 %collective-permute-start = (bf16[1040,512]{1,0:T(8,128)(2,1)S(1)}, bf16[1040,512]{1,0:T(8,128)(2,1)S(1)}, u32[]{:S(2)}, u32[]{:S(2)}) collective-permute-start(bf16[1040,512]{1,0:T(8,128)(2,1)S(1)} %get-tuple-element.37), channel_id=1, source_target_pairs={{0,1},{1,0},{2,3},{3,2},{4,5},{5,4},{6,7},{7,6},{8,9},{9,8},{10,11... | collective-permute-start | bytes 3194888 | tf_op jit(solution)/shard_map/ppermute | solution.py:360
  213.9 9.5 %collective-permute-start.2 = (bf16[1040,128]{1,0:T(8,128)(2,1)S(1)}, bf16[1040,128]{1,0:T(8,128)(2,1)S(1)}, u32[]{:S(2)}, u32[]{:S(2)}) collective-permute-start(bf16[1040,128]{1,0:T(8,128)(2,1)S(1)} %get-tuple-element.42), channel_id=1, source_target_pairs={{0,2},{2,0},{4,6},{6,4},{1,3},{3,1},{5,7},{7,5},{8,10},{10,8},{12,... | collective-permute-start | bytes 798728 | tf_op jit(solution)/shard_map/ppermute | solution.py:373
  216.3 12.8 %collective-permute-start.1 = (bf16[1024,128]{1,0:T(8,128)(2,1)S(1)}, bf16[1024,128]{1,0:T(8,128)(2,1)S(1)}, u32[]{:S(2)}, u32[]{:S(2)}) collective-permute-start(bf16[1024,128]{1,0:T(8,128)(2,1)S(1)} %get-tuple-element.40), channel_id=1, source_target_pairs={{0,2},{2,0},{4,6},{6,4},{1,3},{3,1},{5,7},{7,5},{8,10},{10,8},{12,... | collective-permute-start | bytes 786440 | tf_op jit(solution)/shard_map/ppermute | solution.py:374
  223.5 16.0 %collective-permute-start.3 = (bf16[1040,128]{1,0:T(8,128)(2,1)S(1)}, bf16[1040,128]{1,0:T(8,128)(2,1)S(1)}, u32[]{:S(2)}, u32[]{:S(2)}) collective-permute-start(bf16[1040,128]{1,0:T(8,128)(2,1)S(1)} %get-tuple-element.44), channel_id=1, source_target_pairs={{0,4},{4,0},{2,6},{6,2},{1,5},{5,1},{3,7},{7,3},{8,12},{12,8},{10,... | collective-permute-start | bytes 798728 | tf_op jit(solution)/shard_map/ppermute | solution.py:376
Sparse Core Ops, SparseCore 0:
  66.9 62.7 all-gather.2

commit v4 on v1

--- a/solution.py
+++ b/solution.py
@@ -145,14 +145,18 @@
     col_out[...] = spread(over_items(scale, k), copies)
 
 
-def both_cols_body(copies, gathered, k, k_one, col_out, scale_out, held, sem):
+def both_cols_body(copies, gathered, k, k_one, came, col_out, scale_out, theirs, ours, held, sem, sems, our_sems):
+    core = lax.axis_index("core")
     fetch = pltpu.make_async_copy(k_one, held, sem)
     fetch.start()
+    picks = fetch_parity(came, theirs, 1 - core, sems) + fetch_parity(came, ours, core, our_sems)
     scale = 1.0 / jnp.sum(gathered[...], axis=0)
     scale_out[...] = scale[0:1]
     col_out[:, 0:1, :] = spread(over_items(scale[0:1], k), copies)
     fetch.wait()
     col_out[:, 1:2, :] = spread(over_items(scale[1:2], held), copies)
+    for pick in picks:
+        pick.wait()
 
 
 def row_body(target, groups, cols, k, *refs):
@@ -183,10 +187,9 @@
     return fetches
 
 
-def transport_body(target, cols, r, k, came, t_out, other_out, sums_out, picked, sems):
+def transport_body(target, cols, r, k, theirs, t_out, other_out, sums_out):
     rows, codes = k.shape
     wide = other_out.shape[1]
-    fetches = fetch_parity(came, picked, 1 - lax.axis_index("core"), sems)
     scale = target / jnp.sum(cols[...], axis=0)[0:1]
     sums = over_codes(scale, k)
     sums_out[...] = sums
@@ -194,22 +197,18 @@
     filled = jnp.concatenate([parts, jnp.zeros((16 - parts.shape[0], wide), F32)], 0)
     other_out[rows : rows + 16, :] = filled.astype(BF16)
     r_up = jnp.transpose(jnp.broadcast_to(r[0:1, :], (8, r.shape[1])))
-    for fetch in fetches:
-        fetch.wait()
     for i in range(rows // STEP):
         here = slice(i * STEP, (i + 1) * STEP)
         t = (r_up[here, 0:1] * k[here, :].astype(F32) * scale).astype(BF16)
         t_out[here, :] = t
-        other_out[here, :] = nt(t, picked[...].reshape(wide, codes)).astype(BF16)
-
-
-def mine_body(t, came, out, picked, sems):
+        other_out[here, :] = nt(t, theirs[...].reshape(wide, codes)).astype(BF16)
+
+
+def mine_body(t, ours, out):
     wide = out.shape[1]
-    for fetch in fetch_parity(came, picked, lax.axis_index("core"), sems):
-        fetch.wait()
     for i in range(t.shape[0] // STEP):
         here = slice(i * STEP, (i + 1) * STEP)
-        out[here, :] = nt(t[here, :], picked[...].reshape(wide, t.shape[1]))
+        out[here, :] = nt(t[here, :], ours[...].reshape(wide, t.shape[1]))
 
 
 def pack(sums):
@@ -289,7 +288,7 @@
         "kernel_two",
         [(came_two, HBM), (block_two, HBM)],
         flops=book_flops,
-        limit=MOST,
+        limit=MOST + 4 * MIB - MIB // 4,
         scratch=book_room + [sem((plane + steps,))],
     )
 
@@ -313,14 +312,15 @@
         gathered = lax.all_to_all(row_sums, CODES, 0, 0)
         outs = (shape(plane, n, codes), shape(1, rows))
         if last:
-            col, scale = call(
+            parity = shape(RING, 2, RING, run, codes, of=BF16)
+            col, scale, theirs, ours = call(
                 functools.partial(both_cols_body, plane),
-                outs,
+                outs + (parity, parity),
                 "columns",
-                [gathered, k_two, (k_one, HBM)],
+                [gathered, k_two, (k_one, HBM), (came_two, HBM)],
                 flops=small,
                 limit=MOST,
-                scratch=[pltpu.VMEM((rows, codes), BF16), sem],
+                scratch=[pltpu.VMEM((rows, codes), BF16), sem, sem((plane,)), sem((plane,))],
             )
         else:
             col, scale = call(
@@ -342,25 +342,17 @@
 
     wide = features // 2
     width = features // groups
-    picked = pltpu.VMEM((RING, 2, RING, run, codes), BF16)
     t, other, sums = call(
         functools.partial(transport_body, target),
         (shape(rows, codes, of=BF16), shape(rows + 16, wide, of=BF16), shape(1, rows)),
         "transport",
-        [cols, scale, k_two, (came_two, HBM)],
+        [cols, scale, k_two, theirs],
         flops=book_flops // 2,
-        limit=MOST - 4 * MIB,
-        scratch=[picked, sem((plane,))],
+        limit=24 * MIB,
     )
     came = lax.ppermute(other, "core", [(0, 1), (1, 0)])
     mine = call(
-        mine_body,
-        shape(rows, wide),
-        "mine",
-        [t, (came_two, HBM)],
-        flops=book_flops // 2,
-        limit=MOST - 4 * MIB,
-        scratch=[picked, sem((plane,))],
+        mine_body, shape(rows, wide), "mine", [t, ours], flops=book_flops // 2, limit=24 * MIB
     )
     tall = shape(rows + 16, width, of=BF16)
     own, far, sums, cross, beside = call(
@@ -372,10 +364,9 @@
     )
     neighbours = [(0, 1), (1, 0), (2, 3), (3, 2)]
     crossed = lax.ppermute(cross, "z_lo", neighbours)
+    beside = lax.ppermute(beside, "z_lo", neighbours)
     passed, sums = call(cross_body, (tall, shape(8, width)), "cross", [far, crossed, sums])
-    passed, beside = lax.optimization_barrier((passed, beside))
     passed = lax.ppermute(passed, "z_lo", [(0, 2), (2, 0), (1, 3), (3, 1)])
-    beside = lax.ppermute(beside, "z_lo", neighbours)
     rebuilt = call(
         last_body, shape(rows, width, of=BF16), "last", [own, beside, passed, sums, scale]
     )

time: 246 us -> 246 us (level)
    ppermute x1, waiting for transfers between devices: 4.4 us -> 10.4 us  [shards(): passed = lax.ppermute(passed, 'z_lo', [(0, 2), (2, 0), (1, 3), (3, 1)])]
    ppermute x1, waiting for transfers between devices: 6.73 us -> 2.81 us  [shards(): beside = lax.ppermute(beside, 'z_lo', neighbours)]
    ppermute x1, waiting for transfers between devices: 7.13 us -> 4.2 us  [shards(): crossed = lax.ppermute(cross, 'z_lo', neighbours)]
  transfers between devices with their start and end apart: 6 -> 6, of which waited for: 5 -> 5; matrix products, arithmetic and copies ran while one was open for 1% -> 1% of each run, Pallas kernels for 7% -> 6%
where the time goes in v4:
time: 246 us; the launch traced here: 245 us
  blocking collectives  162 us (66%)
  Pallas kernels  23.9 us (10%)
  waiting for transfers between devices  22.5 us (9%)
  starting transfers between devices  16.3 us (7%)
  between operations  14.2 us (6%)
  local copies, waits for them, and re-layouts  4.14 us (2%)
    all_to_all x3, blocking collectives, shards(): gathered = lax.all_to_all(row_sums, CODES, 0, 0)  43.6 us
    all_to_all x2, blocking collectives, shards(): cols = lax.all_to_all(col, 'z_hi', 0, 0)  32.2 us
    all_to_all x1, blocking collectives, shards(): column = lax.all_to_all(both_books, 'z_hi', 0, 0)  29.6 us
    all_to_all x3, blocking collectives, shards(): col = spread(jnp.sum(lax.all_to_all(col, PLANE, 0, 0), axis=0), RING)  28.7 us
    all_to_all x1, blocking collectives, shards(): came_two = lax.all_to_all(two, PLANE, 0, 0)  28.3 us
    pallas_call x13, Pallas kernels, call(): pl.pallas_call(body, out_shape=outs, in_specs=[spec for _, spec in ins],...  23.9 us
    ppermute x1, waiting for transfers between devices, shards(): passed = lax.ppermute(passed, 'z_lo', [(0, 2), (2, 0), (1, 3), (3, 1)])  10.4 us
    ppermute x1, starting transfers between devices, shards(): came = lax.ppermute(other, 'core', [(0, 1), (1, 0)])  5.62 us
  transfers between devices with their start and end apart: 6, of which 5 were waited for; matrix products, arithmetic and copies ran while one was open for 1% of the time, Pallas kernels for 6%

profile of v4, /device:TPU:1, one launch (start us, length us, event | category | flops | bytes accessed | tf_op | source)
XLA Modules:
  0.0 245.0 jit_solution(4795713645994525206)
XLA Ops:
  8.0 29.6 %all_to_all.55.column = bf16[4,32,1024]{2,1,0:T(8,128)(2,1)S(1)} all-to-all(bf16[4,32,1024]{2,1,0:T(8,128)(2,1)S(1)} %broadcast_in_dim.8), channel_id=1, replica_groups=mesh['x'=4,'z_hi'=4,'y'=4,'z_lo'=4,'core'=2] {'z_hi'}, dimensions={0} | all-to-all | bytes 524288 | tf_op jit(solution)/shard_map/all_to_all | solution.py:271
  38.4 28.3 %all_to_all.56.came = bf16[16,4,16,1024]{3,2,1,0:T(8,128)(2,1)} all-to-all(bf16[16,4,16,1024]{3,2,1,0:T(8,128)(2,1)S(1)} %get-tuple-element.26), channel_id=1, replica_groups=mesh['x'=4,'z_hi'=4,'y'=4,'z_lo'=4,'core'=2] {'x','y'}, dimensions={0} | all-to-all | bytes 4194304 | tf_op jit(solution)/shard_map/all_to_all | solution.py:278
  66.7 5.9 %kernel_two.1 = (bf16[1024,1024]{1,0:T(8,128)(2,1)S(1)}, f32[8,1,1024]{2,1,0:T(1,128)S(1)}) custom-call(bf16[16,4,16,1024]{3,2,1,0:T(8,128)(2,1)} %all_to_all.56.came, bf16[1024,1024]{1,0:T(8,128)(2,1)} %block.2), custom_call_target="tpu_custom_call" | custom-call | flops 2147483648 | bytes 4194304 | tf_op jit(solution)/shard_map/kernel_two/pallas_call | solution.py:28
  72.6 21.8 %all_to_all.57.gathered = f32[8,1,1024]{2,1,0:T(1,128)S(1)} all-to-all(f32[8,1,1024]{2,1,0:T(1,128)S(1)} %get-tuple-element.29), channel_id=1, replica_groups=mesh['x'=4,'z_hi'=4,'y'=4,'z_lo'=4,'core'=2] {'z_lo','core'}, dimensions={0} | all-to-all | bytes 65536 | tf_op jit(solution)/shard_map/all_to_all | solution.py:312
  95.3 9.5 %all_to_all.58 = f32[16,1,1024]{2,1,0:T(1,128)S(1)} all-to-all(f32[16,1,1024]{2,1,0:T(1,128)S(1)} %get-tuple-element.31), channel_id=1, replica_groups=mesh['x'=4,'z_hi'=4,'y'=4,'z_lo'=4,'core'=2] {'x','y'}, dimensions={0} | all-to-all | bytes 131072 | tf_op jit(solution)/shard_map/all_to_all | solution.py:329
  104.8 14.4 %all_to_all.59.cols = f32[4,1,1024]{2,1,0:T(1,128)S(1)} all-to-all(f32[4,1,1024]{2,1,0:T(1,128)S(1)} %broadcast_in_dim.9), channel_id=1, replica_groups=mesh['x'=4,'z_hi'=4,'y'=4,'z_lo'=4,'core'=2] {'z_hi'}, dimensions={0} | all-to-all | bytes 32768 | tf_op jit(solution)/shard_map/all_to_all | solution.py:330
  119.9 11.1 %all_to_all.60.gathered = f32[8,1,1024]{2,1,0:T(1,128)S(1)} all-to-all(f32[8,1,1024]{2,1,0:T(1,128)S(1)} %rows.2), channel_id=1, replica_groups=mesh['x'=4,'z_hi'=4,'y'=4,'z_lo'=4,'core'=2] {'z_lo','core'}, dimensions={0} | all-to-all | bytes 65536 | tf_op jit(solution)/shard_map/all_to_all | solution.py:312
  131.8 9.6 %all_to_all.61 = f32[16,1,1024]{2,1,0:T(1,128)S(1)} all-to-all(f32[16,1,1024]{2,1,0:T(1,128)S(1)} %get-tuple-element.32), channel_id=1, replica_groups=mesh['x'=4,'z_hi'=4,'y'=4,'z_lo'=4,'core'=2] {'x','y'}, dimensions={0} | all-to-all | bytes 131072 | tf_op jit(solution)/shard_map/all_to_all | solution.py:329
  142.1 3.2 %all-to-all-start.7 = ((f32[4,1,1024]{2,1,0:T(1,128)}), f32[4,1,1024]{2,1,0:T(1,128)S(1)}, u32[]{:S(2)}, u32[]{:S(2)}) async-start(f32[4,1,1024]{2,1,0:T(1,128)} %broadcast_in_dim.10.after), calls=%async_computation.7 | async-start | bytes 32768 | tf_op jit(solution)/shard_map/all_to_all | solution.py:330
  145.4 6.0 %kernel_one.1 = (bf16[1024,1024]{1,0:T(8,128)(2,1)S(1)}, f32[8,1,1024]{2,1,0:T(1,128)S(1)}) custom-call(bf16[16,4,16,1024]{3,2,1,0:T(8,128)(2,1)} %bitcast.5, bf16[1024,1024]{1,0:T(8,128)(2,1)} %block.3, f32[4,1,1024]{2,1,0:T(1,128)} %broadcast_in_dim.10.after), custom_call_target="tpu_custom_call" | custom-call | flops 2147483648 | bytes 4194304 | tf_op jit(solution)/shard_map/kernel_one/pallas_call | solution.py:28
  151.4 1.3 copy-done
  152.7 4.0 %all-to-all-done.7.cols = f32[4,1,1024]{2,1,0:T(1,128)S(1)} async-done(((f32[4,1,1024]{2,1,0:T(1,128)}), f32[4,1,1024]{2,1,0:T(1,128)S(1)}, u32[]{:S(2)}, u32[]{:S(2)}) %all-to-all-start.7) | async-done | bytes 16416 | tf_op jit(solution)/shard_map/all_to_all | solution.py:330
  157.4 10.8 %all_to_all.62.gathered = f32[8,2,1024]{2,1,0:T(2,128)S(1)} all-to-all(f32[8,2,1024]{2,1,0:T(2,128)S(1)} %rows.3), channel_id=1, replica_groups=mesh['x'=4,'z_hi'=4,'y'=4,'z_lo'=4,'core'=2] {'z_lo','core'}, dimensions={0} | all-to-all | bytes 131072 | tf_op jit(solution)/shard_map/all_to_all | solution.py:312
  168.2 3.3 %columns.5 = (f32[16,2,1024]{2,1,0:T(2,128)S(1)}, f32[1,1024]{1,0:T(1,128)S(1)}, bf16[4,2,4,16,1024]{4,3,2,1,0:T(8,128)(2,1)S(1)}, bf16[4,2,4,16,1024]{4,3,2,1,0:T(8,128)(2,1)S(1)}) custom-call(f32[8,2,1024]{2,1,0:T(2,128)S(1)} %all_to_all.62.gathered, bf16[1024,1024]{1,0:T(8,128)(2,1)S(1)} %get-tuple-element.30.k, bf16[1024,1024]{1,0:T(8,128)(2,1)} %copy-done, ...), custom_call_target="tpu_custom_call" | custom-call | flops 33554432 | bytes 4194304 | tf_op jit(solution)/shard_map/columns/pallas_call | solution.py:28
  172.5 9.6 %all_to_all.63 = f32[16,2,1024]{2,1,0:T(2,128)S(1)} all-to-all(f32[16,2,1024]{2,1,0:T(2,128)S(1)} %get-tuple-element.36), channel_id=1, replica_groups=mesh['x'=4,'z_hi'=4,'y'=4,'z_lo'=4,'core'=2] {'x','y'}, dimensions={0} | all-to-all | bytes 262144 | tf_op jit(solution)/shard_map/all_to_all | solution.py:329
  182.2 17.8 %all_to_all.64.cols = f32[4,2,1024]{2,1,0:T(2,128)S(1)} all-to-all(f32[4,2,1024]{2,1,0:T(2,128)S(1)} %broadcast_in_dim.11), channel_id=1, replica_groups=mesh['x'=4,'z_hi'=4,'y'=4,'z_lo'=4,'core'=2] {'z_hi'}, dimensions={0} | all-to-all | bytes 65536 | tf_op jit(solution)/shard_map/all_to_all | solution.py:330
  201.3 1.9 transport.1
  203.2 5.6 %collective-permute-start = (bf16[1040,512]{1,0:T(8,128)(2,1)S(1)}, bf16[1040,512]{1,0:T(8,128)(2,1)S(1)}, u32[]{:S(2)}, u32[]{:S(2)}) collective-permute-start(bf16[1040,512]{1,0:T(8,128)(2,1)S(1)} %get-tuple-element.41), channel_id=1, source_target_pairs={{0,1},{1,0},{2,3},{3,2},{4,5},{5,4},{6,7},{7,6},{8,9},{9,8},{10,11... | collective-permute-start | bytes 3194888 | tf_op jit(solution)/shard_map/ppermute | solution.py:353
  211.5 2.4 collective-permute-start.2
  213.9 2.9 %collective-permute-start.1 = (bf16[1024,128]{1,0:T(8,128)(2,1)S(1)}, bf16[1024,128]{1,0:T(8,128)(2,1)S(1)}, u32[]{:S(2)}, u32[]{:S(2)}) collective-permute-start(bf16[1024,128]{1,0:T(8,128)(2,1)S(1)} %get-tuple-element.44), channel_id=1, source_target_pairs={{0,2},{2,0},{4,6},{6,4},{1,3},{3,1},{5,7},{7,5},{8,10},{10,8},{12,... | collective-permute-start | bytes 786440 | tf_op jit(solution)/shard_map/ppermute | solution.py:367
  216.8 4.2 %collective-permute-done.2.came = bf16[1040,128]{1,0:T(8,128)(2,1)S(1)} collective-permute-done((bf16[1040,128]{1,0:T(8,128)(2,1)S(1)}, bf16[1040,128]{1,0:T(8,128)(2,1)S(1)}, u32[]{:S(2)}, u32[]{:S(2)}) %collective-permute-start.2) | collective-permute-done | bytes 266272 | tf_op jit(solution)/shard_map/ppermute | solution.py:366
  221.1 2.1 collective-permute-start.3
  223.9 2.8 %collective-permute-done.1.beside = bf16[1024,128]{1,0:T(8,128)(2,1)S(1)} collective-permute-done((bf16[1024,128]{1,0:T(8,128)(2,1)S(1)}, bf16[1024,128]{1,0:T(8,128)(2,1)S(1)}, u32[]{:S(2)}, u32[]{:S(2)}) %collective-permute-start.1) | collective-permute-done | bytes 262176 | tf_op jit(solution)/shard_map/ppermute | solution.py:367
  226.7 10.4 %collective-permute-done.3.far = bf16[1040,128]{1,0:T(8,128)(2,1)S(1)} collective-permute-done((bf16[1040,128]{1,0:T(8,128)(2,1)S(1)}, bf16[1040,128]{1,0:T(8,128)(2,1)S(1)}, u32[]{:S(2)}, u32[]{:S(2)}) %collective-permute-start.3) | collective-permute-done | bytes 266272 | tf_op jit(solution)/shard_map/ppermute | solution.py:369
  (28 shorter events, 12.2 us)
Async XLA Ops:
  7.2 138.2 %all-gather.3.cloned.1.call-start = ((), (), s32[]{:S(2)}) async-start(), calls=%async_computation.11 | async-start | bytes 2228224 | tf_op jit(solution)/shard_map/all_gather | solution.py:280
  142.1 14.7 %all-to-all-start.7 = ((f32[4,1,1024]{2,1,0:T(1,128)}), f32[4,1,1024]{2,1,0:T(1,128)S(1)}, u32[]{:S(2)}, u32[]{:S(2)}) async-start(f32[4,1,1024]{2,1,0:T(1,128)} %broadcast_in_dim.10.after), calls=%async_computation.7 | async-start | bytes 32768 | tf_op jit(solution)/shard_map/all_to_all | solution.py:330
  151.4 1.3 copy-start
  171.6 1.0 copy-start.1
  200.0 1.2 copy-start.2
  203.2 7.9 %collective-permute-start = (bf16[1040,512]{1,0:T(8,128)(2,1)S(1)}, bf16[1040,512]{1,0:T(8,128)(2,1)S(1)}, u32[]{:S(2)}, u32[]{:S(2)}) collective-permute-start(bf16[1040,512]{1,0:T(8,128)(2,1)S(1)} %get-tuple-element.41), channel_id=1, source_target_pairs={{0,1},{1,0},{2,3},{3,2},{4,5},{5,4},{6,7},{7,6},{8,9},{9,8},{10,11... | collective-permute-start | bytes 3194888 | tf_op jit(solution)/shard_map/ppermute | solution.py:353
  211.5 9.5 %collective-permute-start.2 = (bf16[1040,128]{1,0:T(8,128)(2,1)S(1)}, bf16[1040,128]{1,0:T(8,128)(2,1)S(1)}, u32[]{:S(2)}, u32[]{:S(2)}) collective-permute-start(bf16[1040,128]{1,0:T(8,128)(2,1)S(1)} %get-tuple-element.46), channel_id=1, source_target_pairs={{0,2},{2,0},{4,6},{6,4},{1,3},{3,1},{5,7},{7,5},{8,10},{10,8},{12,... | collective-permute-start | bytes 798728 | tf_op jit(solution)/shard_map/ppermute | solution.py:366
  213.9 12.8 %collective-permute-start.1 = (bf16[1024,128]{1,0:T(8,128)(2,1)S(1)}, bf16[1024,128]{1,0:T(8,128)(2,1)S(1)}, u32[]{:S(2)}, u32[]{:S(2)}) collective-permute-start(bf16[1024,128]{1,0:T(8,128)(2,1)S(1)} %get-tuple-element.44), channel_id=1, source_target_pairs={{0,2},{2,0},{4,6},{6,4},{1,3},{3,1},{5,7},{7,5},{8,10},{10,8},{12,... | collective-permute-start | bytes 786440 | tf_op jit(solution)/shard_map/ppermute | solution.py:367
  221.1 16.0 %collective-permute-start.3 = (bf16[1040,128]{1,0:T(8,128)(2,1)S(1)}, bf16[1040,128]{1,0:T(8,128)(2,1)S(1)}, u32[]{:S(2)}, u32[]{:S(2)}) collective-permute-start(bf16[1040,128]{1,0:T(8,128)(2,1)S(1)} %get-tuple-element.48), channel_id=1, source_target_pairs={{0,4},{4,0},{2,6},{6,2},{1,5},{5,1},{3,7},{7,3},{8,12},{12,8},{10,... | collective-permute-start | bytes 798728 | tf_op jit(solution)/shard_map/ppermute | solution.py:369
Sparse Core Ops, SparseCore 0:
  66.9 62.7 all-gather.2

commit v5 on v1

--- a/solution.py
+++ b/solution.py
@@ -87,14 +87,15 @@
     return 0.5 * jnp.sum(acc, axis=0, keepdims=True)
 
 
-def make_k(inv_root, groups, came, block, k, total, book, held, sems, after_step=None):
-    rows, features = block.shape
+def make_k(inv_root, groups, start, came, block, k, total, book, held, sems, after_step=None):
+    rows, features = held.shape
     codes = book.shape[-1]
     fetches = fetch_book(came, book, sems)
     loads = []
     for i in range(rows // STEP):
         here = pl.ds(i * STEP, STEP)
-        loads.append(pltpu.make_async_copy(block.at[here], held.at[here], sems.at[len(fetches) + i]))
+        there = pl.ds(start + i * STEP, STEP)
+        loads.append(pltpu.make_async_copy(block.at[there], held.at[here], sems.at[len(fetches) + i]))
         loads[-1].start()
     norms = half_norms(book, fetches)
     ones = jnp.ones((16, codes), BF16)
@@ -109,10 +110,10 @@
 
 
 def kernel_two_body(inv_root, groups, came, block, k_out, total, book, held, sems):
-    make_k(inv_root, groups, came, block, k_out, total, book, held, sems)
-
-
-def kernel_one_body(inv_root, groups, came, block, after, k_out, total, book, held, k, sems, saved):
+    make_k(inv_root, groups, 0, came, block, k_out, total, book, held, sems)
+
+
+def kernel_one_body(inv_root, groups, start, came, block, after, k_out, total, book, held, k, sems, saved):
     saves = []
 
     def save(i):
@@ -120,7 +121,7 @@
         saves.append(pltpu.make_async_copy(k.at[here], k_out.at[here], saved.at[i]))
         saves[-1].start()
 
-    make_k(inv_root, groups, came, block, k, total, book, held, sems, save)
+    make_k(inv_root, groups, start, came, block, k, total, book, held, sems, save)
     for move in saves:
         move.wait()
 
@@ -145,13 +146,17 @@
     col_out[...] = spread(over_items(scale, k), copies)
 
 
-def both_cols_body(copies, gathered, k, k_one, col_out, scale_out, held, sem):
-    fetch = pltpu.make_async_copy(k_one, held, sem)
-    fetch.start()
+def both_cols_body(copies, gathered, k, first, second, col_out, scale_out, held, sems):
+    half = first.shape[0]
+    fetches = []
+    for i, part in enumerate((first, second)):
+        fetches.append(pltpu.make_async_copy(part, held.at[pl.ds(i * half, half)], sems.at[i]))
+        fetches[-1].start()
     scale = 1.0 / jnp.sum(gathered[...], axis=0)
     scale_out[...] = scale[0:1]
     col_out[:, 0:1, :] = spread(over_items(scale[0:1], k), copies)
-    fetch.wait()
+    for fetch in fetches:
+        fetch.wait()
     col_out[:, 1:2, :] = spread(over_items(scale[1:2], held), copies)
 
 
@@ -159,8 +164,10 @@
     out = refs[-1]
     scale = target / jnp.sum(cols[...], axis=0)[0:1]
     out[:, 0:1, :] = spread(over_codes(scale, k), groups)
+    at = 0
     for more in refs[:-1]:
-        out[:, 1:2, :] = more[...]
+        out[:, 1:2, at : at + more.shape[2]] = more[...]
+        at += more.shape[2]
 
 
 def halves(row):
@@ -172,30 +179,24 @@
     return jnp.concatenate([row[:, i : i + width] for i in range(0, row.shape[1], width)], 0)
 
 
-def fetch_parity(came, picked, parity, sems):
-    fetches = []
+def pick(came, picked, parity):
     for x in range(RING):
         for y in range(RING):
-            here = came.at[x * RING + y, pl.ds(2 * parity, 2)]
-            move = pltpu.make_async_copy(here, picked.at[x, :, y], sems.at[x * RING + y])
-            move.start()
-            fetches.append(move)
-    return fetches
-
-
-def transport_body(target, cols, r, k, came, t_out, other_out, sums_out, picked, sems):
+            for z in range(2):
+                picked[x, z, y] = came[x * RING + y, 2 * parity + z]
+
+
+def transport_body(target, cols, r, k, came, t_out, other_out, sums_out, picked):
     rows, codes = k.shape
     wide = other_out.shape[1]
-    fetches = fetch_parity(came, picked, 1 - lax.axis_index("core"), sems)
     scale = target / jnp.sum(cols[...], axis=0)[0:1]
     sums = over_codes(scale, k)
     sums_out[...] = sums
+    pick(came, picked, 1 - lax.axis_index("core"))
     parts = jnp.concatenate([cut(part.astype(F32), wide) for part in halves(sums)], 0)
     filled = jnp.concatenate([parts, jnp.zeros((16 - parts.shape[0], wide), F32)], 0)
     other_out[rows : rows + 16, :] = filled.astype(BF16)
     r_up = jnp.transpose(jnp.broadcast_to(r[0:1, :], (8, r.shape[1])))
-    for fetch in fetches:
-        fetch.wait()
     for i in range(rows // STEP):
         here = slice(i * STEP, (i + 1) * STEP)
         t = (r_up[here, 0:1] * k[here, :].astype(F32) * scale).astype(BF16)
@@ -203,10 +204,9 @@
         other_out[here, :] = nt(t, picked[...].reshape(wide, codes)).astype(BF16)
 
 
-def mine_body(t, came, out, picked, sems):
+def mine_body(t, came, out, picked):
     wide = out.shape[1]
-    for fetch in fetch_parity(came, picked, lax.axis_index("core"), sems):
-        fetch.wait()
+    pick(came, picked, lax.axis_index("core"))
     for i in range(t.shape[0] // STEP):
         here = slice(i * STEP, (i + 1) * STEP)
         out[here, :] = nt(t[here, :], picked[...].reshape(wide, t.shape[1]))
@@ -289,19 +289,27 @@
         "kernel_two",
         [(came_two, HBM), (block_two, HBM)],
         flops=book_flops,
-        limit=MOST,
+        limit=MOST + 4 * MIB - MIB // 4,
         scratch=book_room + [sem((plane + steps,))],
     )
 
-    def make_k_one(after):
+    half = rows // 2
+
+    def make_k_one(start, after):
         return call(
-            functools.partial(kernel_one_body, inv_root, groups),
-            (shape(rows, codes, of=BF16), shape(groups, 1, rows)),
+            functools.partial(kernel_one_body, inv_root, groups, start),
+            (shape(half, codes, of=BF16), shape(groups, 1, half)),
             "kernel_one",
             [(came_one, HBM), (block_one, HBM), (after, HBM)],
-            flops=book_flops,
-            limit=MOST + 2 * MIB,
-            scratch=book_room + [pltpu.VMEM((rows, codes), BF16), sem((plane + steps,)), sem((steps,))],
+            flops=book_flops // 2,
+            limit=MOST + 4 * MIB,
+            scratch=[
+                book_room[0],
+                pltpu.VMEM((half, features), BF16),
+                pltpu.VMEM((half, codes), BF16),
+                sem((plane + steps // 2,)),
+                sem((steps // 2,)),
+            ],
             out_specs=(HBM, FULL),
         )
 
@@ -317,24 +325,28 @@
                 functools.partial(both_cols_body, plane),
                 outs,
                 "columns",
-                [gathered, k_two, (k_one, HBM)],
+                [gathered, k_two] + [(part, HBM) for part in k_one],
                 flops=small,
                 limit=MOST,
-                scratch=[pltpu.VMEM((rows, codes), BF16), sem],
+                scratch=[pltpu.VMEM((rows, codes), BF16), sem((2,))],
             )
         else:
             col, scale = call(
                 functools.partial(col_body, plane), outs, "columns", [gathered, k_two], flops=small
             )
-        col = spread(jnp.sum(lax.all_to_all(col, PLANE, 0, 0), axis=0), RING)
+        col_all = lax.all_to_all(col, PLANE, 0, 0)
+        if sweep == 1:
+            first_k, first_one = make_k_one(0, col)
+            col_all, first_one = lax.optimization_barrier((col_all, first_one))
+        col = spread(jnp.sum(col_all, axis=0), RING)
         cols = lax.all_to_all(col, "z_hi", 0, 0)
         if sweep == 1:
-            k_one, first_one = make_k_one(col)
-            more = [first_one]
+            second_k, second_one = make_k_one(half, col)
+            k_one, more = [first_k, second_k], [first_one, second_one]
         if not last:
             row_sums = call(
                 functools.partial(row_body, target, groups),
-                shape(groups, 1 + len(more), rows),
+                shape(groups, 2 if more else 1, rows),
                 "rows",
                 [cols, k_two] + more,
                 flops=small,
@@ -342,25 +354,24 @@
 
     wide = features // 2
     width = features // groups
-    picked = pltpu.VMEM((RING, 2, RING, run, codes), BF16)
     t, other, sums = call(
         functools.partial(transport_body, target),
         (shape(rows, codes, of=BF16), shape(rows + 16, wide, of=BF16), shape(1, rows)),
         "transport",
-        [cols, scale, k_two, (came_two, HBM)],
+        [cols, scale, k_two, came_two],
         flops=book_flops // 2,
-        limit=MOST - 4 * MIB,
-        scratch=[picked, sem((plane,))],
+        limit=24 * MIB,
+        scratch=[pltpu.VMEM((RING, 2, RING, run, codes), BF16)],
     )
     came = lax.ppermute(other, "core", [(0, 1), (1, 0)])
     mine = call(
         mine_body,
         shape(rows, wide),
         "mine",
-        [t, (came_two, HBM)],
+        [t, came_two],
         flops=book_flops // 2,
-        limit=MOST - 4 * MIB,
-        scratch=[picked, sem((plane,))],
+        limit=24 * MIB,
+        scratch=[pltpu.VMEM((RING, 2, RING, run, codes), BF16)],
     )
     tall = shape(rows + 16, width, of=BF16)
     own, far, sums, cross, beside = call(
@@ -372,10 +383,9 @@
     )
     neighbours = [(0, 1), (1, 0), (2, 3), (3, 2)]
     crossed = lax.ppermute(cross, "z_lo", neighbours)
+    beside = lax.ppermute(beside, "z_lo", neighbours)
     passed, sums = call(cross_body, (tall, shape(8, width)), "cross", [far, crossed, sums])
-    passed, beside = lax.optimization_barrier((passed, beside))
     passed = lax.ppermute(passed, "z_lo", [(0, 2), (2, 0), (1, 3), (3, 1)])
-    beside = lax.ppermute(beside, "z_lo", neighbours)
     rebuilt = call(
         last_body, shape(rows, width, of=BF16), "last", [own, beside, passed, sums, scale]
     )

time: 246 us -> 243 us (0.988)
  blocking collectives: 162 us -> 152 us
  waiting for transfers between devices: 22.4 us -> 27.4 us
  starting transfers between devices: 16.2 us -> 20.2 us
    all_to_all x3 -> x2, blocking collectives: 28.6 us -> 20.6 us  [shards(): col_all = lax.all_to_all(col, PLANE, 0, 0)]
    ppermute x1, waiting for transfers between devices: 4.4 us -> 10.4 us  [shards(): passed = lax.ppermute(passed, 'z_lo', [(0, 2), (2, 0), (1, 3), (3, 1)])]
    ppermute x1, waiting for transfers between devices: 6.73 us -> 2.81 us  [shards(): beside = lax.ppermute(beside, 'z_lo', neighbours)]
    all_to_all x0 -> x1, starting transfers between devices: none -> 3.5 us  [shards(): col_all = lax.all_to_all(col, PLANE, 0, 0)]
    ppermute x1, waiting for transfers between devices: 7.13 us -> 4.2 us  [shards(): crossed = lax.ppermute(cross, 'z_lo', neighbours)]
    all_to_all x2, blocking collectives: 32.4 us -> 29.8 us  [shards(): cols = lax.all_to_all(col, 'z_hi', 0, 0)]
    all_to_all x1, waiting for transfers between devices: 4.01 us -> 6.48 us  [shards(): cols = lax.all_to_all(col, 'z_hi', 0, 0)]
    pallas_call x13 -> x14, Pallas kernels: 23.3 us -> 23.5 us  [call(): pl.pallas_call(body, out_shape=outs, in_specs=[spec for _, spec in ins],...]
  transfers between devices with their start and end apart: 6 -> 7, of which waited for: 5 -> 6; matrix products, arithmetic and copies ran while one was open for 1% -> 0% of each run, Pallas kernels for 7% -> 7%
where the time goes in v5:
time: 243 us; the launch traced here: 242 us
  blocking collectives  152 us (63%)
  waiting for transfers between devices  27.4 us (11%)
  Pallas kernels  23.5 us (10%)
  starting transfers between devices  20.2 us (8%)
  between operations  14.2 us (6%)
  local copies, waits for them, and re-layouts  3.22 us (1%)
    all_to_all x3, blocking collectives, shards(): gathered = lax.all_to_all(row_sums, CODES, 0, 0)  43.3 us
    all_to_all x2, blocking collectives, shards(): cols = lax.all_to_all(col, 'z_hi', 0, 0)  29.8 us
    all_to_all x1, blocking collectives, shards(): column = lax.all_to_all(both_books, 'z_hi', 0, 0)  29.6 us
    all_to_all x1, blocking collectives, shards(): came_two = lax.all_to_all(two, PLANE, 0, 0)  28.3 us
    pallas_call x14, Pallas kernels, call(): pl.pallas_call(body, out_shape=outs, in_specs=[spec for _, spec in ins],...  23.5 us
    all_to_all x2, blocking collectives, shards(): col_all = lax.all_to_all(col, PLANE, 0, 0)  20.6 us
    ppermute x1, waiting for transfers between devices, shards(): passed = lax.ppermute(passed, 'z_lo', [(0, 2), (2, 0), (1, 3), (3, 1)])  10.4 us
    all_to_all x1, waiting for transfers between devices, shards(): cols = lax.all_to_all(col, 'z_hi', 0, 0)  6.48 us
  transfers between devices with their start and end apart: 7, of which 6 were waited for; matrix products, arithmetic and copies ran while one was open for 0% of the time, Pallas kernels for 7%

profile of v5, /device:TPU:1, one launch (start us, length us, event | category | flops | bytes accessed | tf_op | source)
XLA Modules:
  0.0 241.7 jit_solution(6154785121609297312)
XLA Ops:
  8.0 29.6 %all_to_all.55.column = bf16[4,32,1024]{2,1,0:T(8,128)(2,1)S(1)} all-to-all(bf16[4,32,1024]{2,1,0:T(8,128)(2,1)S(1)} %broadcast_in_dim.8), channel_id=1, replica_groups=mesh['x'=4,'z_hi'=4,'y'=4,'z_lo'=4,'core'=2] {'z_hi'}, dimensions={0} | all-to-all | bytes 524288 | tf_op jit(solution)/shard_map/all_to_all | solution.py:272
  38.4 28.3 %all_to_all.56.came = bf16[16,4,16,1024]{3,2,1,0:T(8,128)(2,1)} all-to-all(bf16[16,4,16,1024]{3,2,1,0:T(8,128)(2,1)S(1)} %get-tuple-element.28), channel_id=1, replica_groups=mesh['x'=4,'z_hi'=4,'y'=4,'z_lo'=4,'core'=2] {'x','y'}, dimensions={0} | all-to-all | bytes 4194304 | tf_op jit(solution)/shard_map/all_to_all | solution.py:279
  66.7 5.9 %kernel_two.1 = (bf16[1024,1024]{1,0:T(8,128)(2,1)S(1)}, f32[8,1,1024]{2,1,0:T(1,128)S(1)}) custom-call(bf16[16,4,16,1024]{3,2,1,0:T(8,128)(2,1)} %all_to_all.56.came, bf16[1024,1024]{1,0:T(8,128)(2,1)} %block.3), custom_call_target="tpu_custom_call" | custom-call | flops 2147483648 | bytes 4194304 | tf_op jit(solution)/shard_map/kernel_two/pallas_call | solution.py:28
  72.6 21.8 %all_to_all.57.gathered = f32[8,1,1024]{2,1,0:T(1,128)S(1)} all-to-all(f32[8,1,1024]{2,1,0:T(1,128)S(1)} %get-tuple-element.31), channel_id=1, replica_groups=mesh['x'=4,'z_hi'=4,'y'=4,'z_lo'=4,'core'=2] {'z_lo','core'}, dimensions={0} | all-to-all | bytes 65536 | tf_op jit(solution)/shard_map/all_to_all | solution.py:321
  95.3 9.5 %all_to_all.58 = f32[16,1,1024]{2,1,0:T(1,128)S(1)} all-to-all(f32[16,1,1024]{2,1,0:T(1,128)S(1)} %get-tuple-element.33), channel_id=1, replica_groups=mesh['x'=4,'z_hi'=4,'y'=4,'z_lo'=4,'core'=2] {'x','y'}, dimensions={0} | all-to-all | bytes 131072 | tf_op jit(solution)/shard_map/all_to_all | solution.py:337
  104.8 14.4 %all_to_all.59.cols = f32[4,1,1024]{2,1,0:T(1,128)S(1)} all-to-all(f32[4,1,1024]{2,1,0:T(1,128)S(1)} %broadcast_in_dim.9), channel_id=1, replica_groups=mesh['x'=4,'z_hi'=4,'y'=4,'z_lo'=4,'core'=2] {'z_hi'}, dimensions={0} | all-to-all | bytes 32768 | tf_op jit(solution)/shard_map/all_to_all | solution.py:342
  119.9 11.1 %all_to_all.60.gathered = f32[8,1,1024]{2,1,0:T(1,128)S(1)} all-to-all(f32[8,1,1024]{2,1,0:T(1,128)S(1)} %rows.2), channel_id=1, replica_groups=mesh['x'=4,'z_hi'=4,'y'=4,'z_lo'=4,'core'=2] {'z_lo','core'}, dimensions={0} | all-to-all | bytes 65536 | tf_op jit(solution)/shard_map/all_to_all | solution.py:321
  132.0 3.5 %all-to-all-start.6 = ((f32[16,1,1024]{2,1,0:T(1,128)}), f32[16,1,1024]{2,1,0:T(1,128)S(1)}, u32[]{:S(2)}, u32[]{:S(2)}) async-start(f32[16,1,1024]{2,1,0:T(1,128)} %get-tuple-element.34.after), calls=%async_computation.6 | async-start | bytes 131072 | tf_op jit(solution)/shard_map/all_to_all | solution.py:337
  135.5 4.0 %kernel_one.2 = (bf16[512,1024]{1,0:T(8,128)(2,1)S(1)}, f32[8,1,512]{2,1,0:T(1,128)S(1)}) custom-call(bf16[16,4,16,1024]{3,2,1,0:T(8,128)(2,1)} %bitcast.3, bf16[1024,1024]{1,0:T(8,128)(2,1)} %block.5, f32[16,1,1024]{2,1,0:T(1,128)} %get-tuple-element.34.after), custom_call_target="tpu_custom_call" | custom-call | flops 1073741824 | bytes 4194304 | tf_op jit(solution)/shard_map/kernel_one/pallas_call | solution.py:28
  139.5 2.4 %all-to-all-done.6 = f32[16,1,1024]{2,1,0:T(1,128)S(1)} async-done(((f32[16,1,1024]{2,1,0:T(1,128)}), f32[16,1,1024]{2,1,0:T(1,128)S(1)}, u32[]{:S(2)}, u32[]{:S(2)}) %all-to-all-start.6) | async-done | bytes 65568 | tf_op jit(solution)/shard_map/all_to_all | solution.py:337
  142.6 3.6 %all-to-all-start.7 = ((f32[4,1,1024]{2,1,0:T(1,128)}), f32[4,1,1024]{2,1,0:T(1,128)S(1)}, u32[]{:S(2)}, u32[]{:S(2)}) async-start(f32[4,1,1024]{2,1,0:T(1,128)} %broadcast_in_dim.10.after), calls=%async_computation.7 | async-start | bytes 32768 | tf_op jit(solution)/shard_map/all_to_all | solution.py:342
  146.2 4.0 %kernel_one.3 = (bf16[512,1024]{1,0:T(8,128)(2,1)S(1)}, f32[8,1,512]{2,1,0:T(1,128)S(1)}) custom-call(bf16[16,4,16,1024]{3,2,1,0:T(8,128)(2,1)} %bitcast.4, bf16[1024,1024]{1,0:T(8,128)(2,1)} %block.5, f32[4,1,1024]{2,1,0:T(1,128)} %broadcast_in_dim.10.after), custom_call_target="tpu_custom_call" | custom-call | flops 1073741824 | bytes 4194304 | tf_op jit(solution)/shard_map/kernel_one/pallas_call | solution.py:28
  151.2 6.5 %all-to-all-done.7.cols = f32[4,1,1024]{2,1,0:T(1,128)S(1)} async-done(((f32[4,1,1024]{2,1,0:T(1,128)}), f32[4,1,1024]{2,1,0:T(1,128)S(1)}, u32[]{:S(2)}, u32[]{:S(2)}) %all-to-all-start.7) | async-done | bytes 16416 | tf_op jit(solution)/shard_map/all_to_all | solution.py:342
  158.4 10.5 %all_to_all.61.gathered = f32[8,2,1024]{2,1,0:T(2,128)S(1)} all-to-all(f32[8,2,1024]{2,1,0:T(2,128)S(1)} %rows.3), channel_id=1, replica_groups=mesh['x'=4,'z_hi'=4,'y'=4,'z_lo'=4,'core'=2] {'z_lo','core'}, dimensions={0} | all-to-all | bytes 131072 | tf_op jit(solution)/shard_map/all_to_all | solution.py:321
  169.8 11.1 %all_to_all.62 = f32[16,2,1024]{2,1,0:T(2,128)S(1)} all-to-all(f32[16,2,1024]{2,1,0:T(2,128)S(1)} %get-tuple-element.42), channel_id=1, replica_groups=mesh['x'=4,'z_hi'=4,'y'=4,'z_lo'=4,'core'=2] {'x','y'}, dimensions={0} | all-to-all | bytes 262144 | tf_op jit(solution)/shard_map/all_to_all | solution.py:337
  181.0 15.4 %all_to_all.63.cols = f32[4,2,1024]{2,1,0:T(2,128)S(1)} all-to-all(f32[4,2,1024]{2,1,0:T(2,128)S(1)} %broadcast_in_dim.11), channel_id=1, replica_groups=mesh['x'=4,'z_hi'=4,'y'=4,'z_lo'=4,'core'=2] {'z_hi'}, dimensions={0} | all-to-all | bytes 65536 | tf_op jit(solution)/shard_map/all_to_all | solution.py:342
  198.0 1.9 transport.1
  200.0 5.6 %collective-permute-start = (bf16[1040,512]{1,0:T(8,128)(2,1)S(1)}, bf16[1040,512]{1,0:T(8,128)(2,1)S(1)}, u32[]{:S(2)}, u32[]{:S(2)}) collective-permute-start(bf16[1040,512]{1,0:T(8,128)(2,1)S(1)} %get-tuple-element.45), channel_id=1, source_target_pairs={{0,1},{1,0},{2,3},{3,2},{4,5},{5,4},{6,7},{7,6},{8,9},{9,8},{10,11... | collective-permute-start | bytes 3194888 | tf_op jit(solution)/shard_map/ppermute | solution.py:366
  208.3 2.4 collective-permute-start.2
  210.7 2.9 %collective-permute-start.1 = (bf16[1024,128]{1,0:T(8,128)(2,1)S(1)}, bf16[1024,128]{1,0:T(8,128)(2,1)S(1)}, u32[]{:S(2)}, u32[]{:S(2)}) collective-permute-start(bf16[1024,128]{1,0:T(8,128)(2,1)S(1)} %get-tuple-element.48), channel_id=1, source_target_pairs={{0,2},{2,0},{4,6},{6,4},{1,3},{3,1},{5,7},{7,5},{8,10},{10,8},{12,... | collective-permute-start | bytes 786440 | tf_op jit(solution)/shard_map/ppermute | solution.py:386
  213.6 4.2 %collective-permute-done.2.came = bf16[1040,128]{1,0:T(8,128)(2,1)S(1)} collective-permute-done((bf16[1040,128]{1,0:T(8,128)(2,1)S(1)}, bf16[1040,128]{1,0:T(8,128)(2,1)S(1)}, u32[]{:S(2)}, u32[]{:S(2)}) %collective-permute-start.2) | collective-permute-done | bytes 266272 | tf_op jit(solution)/shard_map/ppermute | solution.py:385
  217.9 2.1 collective-permute-start.3
  220.6 2.8 %collective-permute-done.1.beside = bf16[1024,128]{1,0:T(8,128)(2,1)S(1)} collective-permute-done((bf16[1024,128]{1,0:T(8,128)(2,1)S(1)}, bf16[1024,128]{1,0:T(8,128)(2,1)S(1)}, u32[]{:S(2)}, u32[]{:S(2)}) %collective-permute-start.1) | collective-permute-done | bytes 262176 | tf_op jit(solution)/shard_map/ppermute | solution.py:386
  223.4 10.4 %collective-permute-done.3.far = bf16[1040,128]{1,0:T(8,128)(2,1)S(1)} collective-permute-done((bf16[1040,128]{1,0:T(8,128)(2,1)S(1)}, bf16[1040,128]{1,0:T(8,128)(2,1)S(1)}, u32[]{:S(2)}, u32[]{:S(2)}) %collective-permute-start.3) | collective-permute-done | bytes 266272 | tf_op jit(solution)/shard_map/ppermute | solution.py:388
  (30 shorter events, 13.7 us)
Async XLA Ops:
  7.2 128.3 %all-gather.3.cloned.1.call-start = ((), (), s32[]{:S(2)}) async-start(), calls=%async_computation.11 | async-start | bytes 2228224 | tf_op jit(solution)/shard_map/all_gather | solution.py:281
  132.0 10.0 %all-to-all-start.6 = ((f32[16,1,1024]{2,1,0:T(1,128)}), f32[16,1,1024]{2,1,0:T(1,128)S(1)}, u32[]{:S(2)}, u32[]{:S(2)}) async-start(f32[16,1,1024]{2,1,0:T(1,128)} %get-tuple-element.34.after), calls=%async_computation.6 | async-start | bytes 131072 | tf_op jit(solution)/shard_map/all_to_all | solution.py:337
  142.6 15.1 %all-to-all-start.7 = ((f32[4,1,1024]{2,1,0:T(1,128)}), f32[4,1,1024]{2,1,0:T(1,128)S(1)}, u32[]{:S(2)}, u32[]{:S(2)}) async-start(f32[4,1,1024]{2,1,0:T(1,128)} %broadcast_in_dim.10.after), calls=%async_computation.7 | async-start | bytes 32768 | tf_op jit(solution)/shard_map/all_to_all | solution.py:342
  150.2 1.0 copy-start.1
  157.7 11.1 %copy-start.2 = (bf16[512,1024]{1,0:T(8,128)(2,1)S(1)}, bf16[512,1024]{1,0:T(8,128)(2,1)}, u32[]{:S(2)}) copy-start(bf16[512,1024]{1,0:T(8,128)(2,1)} %copy-done.1) | copy-start | bytes 3145732
  196.4 1.6 copy-start
  200.0 7.9 %collective-permute-start = (bf16[1040,512]{1,0:T(8,128)(2,1)S(1)}, bf16[1040,512]{1,0:T(8,128)(2,1)S(1)}, u32[]{:S(2)}, u32[]{:S(2)}) collective-permute-start(bf16[1040,512]{1,0:T(8,128)(2,1)S(1)} %get-tuple-element.45), channel_id=1, source_target_pairs={{0,1},{1,0},{2,3},{3,2},{4,5},{5,4},{6,7},{7,6},{8,9},{9,8},{10,11... | collective-permute-start | bytes 3194888 | tf_op jit(solution)/shard_map/ppermute | solution.py:366
  208.3 9.5 %collective-permute-start.2 = (bf16[1040,128]{1,0:T(8,128)(2,1)S(1)}, bf16[1040,128]{1,0:T(8,128)(2,1)S(1)}, u32[]{:S(2)}, u32[]{:S(2)}) collective-permute-start(bf16[1040,128]{1,0:T(8,128)(2,1)S(1)} %get-tuple-element.50), channel_id=1, source_target_pairs={{0,2},{2,0},{4,6},{6,4},{1,3},{3,1},{5,7},{7,5},{8,10},{10,8},{12,... | collective-permute-start | bytes 798728 | tf_op jit(solution)/shard_map/ppermute | solution.py:385
  210.7 12.8 %collective-permute-start.1 = (bf16[1024,128]{1,0:T(8,128)(2,1)S(1)}, bf16[1024,128]{1,0:T(8,128)(2,1)S(1)}, u32[]{:S(2)}, u32[]{:S(2)}) collective-permute-start(bf16[1024,128]{1,0:T(8,128)(2,1)S(1)} %get-tuple-element.48), channel_id=1, source_target_pairs={{0,2},{2,0},{4,6},{6,4},{1,3},{3,1},{5,7},{7,5},{8,10},{10,8},{12,... | collective-permute-start | bytes 786440 | tf_op jit(solution)/shard_map/ppermute | solution.py:386
  217.9 16.0 %collective-permute-start.3 = (bf16[1040,128]{1,0:T(8,128)(2,1)S(1)}, bf16[1040,128]{1,0:T(8,128)(2,1)S(1)}, u32[]{:S(2)}, u32[]{:S(2)}) collective-permute-start(bf16[1040,128]{1,0:T(8,128)(2,1)S(1)} %get-tuple-element.52), channel_id=1, source_target_pairs={{0,4},{4,0},{2,6},{6,2},{1,5},{5,1},{3,7},{7,3},{8,12},{12,8},{10,... | collective-permute-start | bytes 798728 | tf_op jit(solution)/shard_map/ppermute | solution.py:388
Sparse Core Ops, SparseCore 0:
  66.9 62.7 all-gather.2

commit v6 on v5

--- a/solution.py
+++ b/solution.py
@@ -327,7 +327,7 @@
                 "columns",
                 [gathered, k_two] + [(part, HBM) for part in k_one],
                 flops=small,
-                limit=MOST,
+                limit=24 * MIB,
                 scratch=[pltpu.VMEM((rows, codes), BF16), sem((2,))],
             )
         else:

time: 243 us -> 243 us (level)
  no operation moved by 1% of the time
where the time goes in v6:
time: 243 us; the launch traced here: 242 us
  blocking collectives  152 us (63%)
  waiting for transfers between devices  27.4 us (11%)
  Pallas kernels  23.5 us (10%)
  starting transfers between devices  20.2 us (8%)
  between operations  14.2 us (6%)
  local copies, waits for them, and re-layouts  3.22 us (1%)
    all_to_all x3, blocking collectives, shards(): gathered = lax.all_to_all(row_sums, CODES, 0, 0)  43.3 us
    all_to_all x2, blocking collectives, shards(): cols = lax.all_to_all(col, 'z_hi', 0, 0)  29.8 us
    all_to_all x1, blocking collectives, shards(): column = lax.all_to_all(both_books, 'z_hi', 0, 0)  29.6 us
    all_to_all x1, blocking collectives, shards(): came_two = lax.all_to_all(two, PLANE, 0, 0)  28.3 us
    pallas_call x14, Pallas kernels, call(): pl.pallas_call(body, out_shape=outs, in_specs=[spec for _, spec in ins],...  23.5 us
    all_to_all x2, blocking collectives, shards(): col_all = lax.all_to_all(col, PLANE, 0, 0)  20.6 us
    ppermute x1, waiting for transfers between devices, shards(): passed = lax.ppermute(passed, 'z_lo', [(0, 2), (2, 0), (1, 3), (3, 1)])  10.4 us
    all_to_all x1, waiting for transfers between devices, shards(): cols = lax.all_to_all(col, 'z_hi', 0, 0)  6.48 us
  transfers between devices with their start and end apart: 7, of which 6 were waited for; matrix products, arithmetic and copies ran while one was open for 0% of the time, Pallas kernels for 7%

profile of v6, /device:TPU:1, one launch (start us, length us, event | category | flops | bytes accessed | tf_op | source)
XLA Modules:
  0.0 241.7 jit_solution(11405037758944596224)
XLA Ops:
  8.0 29.6 %all_to_all.55.column = bf16[4,32,1024]{2,1,0:T(8,128)(2,1)S(1)} all-to-all(bf16[4,32,1024]{2,1,0:T(8,128)(2,1)S(1)} %broadcast_in_dim.8), channel_id=1, replica_groups=mesh['x'=4,'z_hi'=4,'y'=4,'z_lo'=4,'core'=2] {'z_hi'}, dimensions={0} | all-to-all | bytes 524288 | tf_op jit(solution)/shard_map/all_to_all | solution.py:272
  38.4 28.3 %all_to_all.56.came = bf16[16,4,16,1024]{3,2,1,0:T(8,128)(2,1)} all-to-all(bf16[16,4,16,1024]{3,2,1,0:T(8,128)(2,1)S(1)} %get-tuple-element.28), channel_id=1, replica_groups=mesh['x'=4,'z_hi'=4,'y'=4,'z_lo'=4,'core'=2] {'x','y'}, dimensions={0} | all-to-all | bytes 4194304 | tf_op jit(solution)/shard_map/all_to_all | solution.py:279
  66.7 5.9 %kernel_two.1 = (bf16[1024,1024]{1,0:T(8,128)(2,1)S(1)}, f32[8,1,1024]{2,1,0:T(1,128)S(1)}) custom-call(bf16[16,4,16,1024]{3,2,1,0:T(8,128)(2,1)} %all_to_all.56.came, bf16[1024,1024]{1,0:T(8,128)(2,1)} %block.3), custom_call_target="tpu_custom_call" | custom-call | flops 2147483648 | bytes 4194304 | tf_op jit(solution)/shard_map/kernel_two/pallas_call | solution.py:28
  72.6 21.8 %all_to_all.57.gathered = f32[8,1,1024]{2,1,0:T(1,128)S(1)} all-to-all(f32[8,1,1024]{2,1,0:T(1,128)S(1)} %get-tuple-element.31), channel_id=1, replica_groups=mesh['x'=4,'z_hi'=4,'y'=4,'z_lo'=4,'core'=2] {'z_lo','core'}, dimensions={0} | all-to-all | bytes 65536 | tf_op jit(solution)/shard_map/all_to_all | solution.py:321
  95.3 9.5 %all_to_all.58 = f32[16,1,1024]{2,1,0:T(1,128)S(1)} all-to-all(f32[16,1,1024]{2,1,0:T(1,128)S(1)} %get-tuple-element.33), channel_id=1, replica_groups=mesh['x'=4,'z_hi'=4,'y'=4,'z_lo'=4,'core'=2] {'x','y'}, dimensions={0} | all-to-all | bytes 131072 | tf_op jit(solution)/shard_map/all_to_all | solution.py:337
  104.8 14.4 %all_to_all.59.cols = f32[4,1,1024]{2,1,0:T(1,128)S(1)} all-to-all(f32[4,1,1024]{2,1,0:T(1,128)S(1)} %broadcast_in_dim.9), channel_id=1, replica_groups=mesh['x'=4,'z_hi'=4,'y'=4,'z_lo'=4,'core'=2] {'z_hi'}, dimensions={0} | all-to-all | bytes 32768 | tf_op jit(solution)/shard_map/all_to_all | solution.py:342
  119.9 11.1 %all_to_all.60.gathered = f32[8,1,1024]{2,1,0:T(1,128)S(1)} all-to-all(f32[8,1,1024]{2,1,0:T(1,128)S(1)} %rows.2), channel_id=1, replica_groups=mesh['x'=4,'z_hi'=4,'y'=4,'z_lo'=4,'core'=2] {'z_lo','core'}, dimensions={0} | all-to-all | bytes 65536 | tf_op jit(solution)/shard_map/all_to_all | solution.py:321
  132.0 3.5 %all-to-all-start.6 = ((f32[16,1,1024]{2,1,0:T(1,128)}), f32[16,1,1024]{2,1,0:T(1,128)S(1)}, u32[]{:S(2)}, u32[]{:S(2)}) async-start(f32[16,1,1024]{2,1,0:T(1,128)} %get-tuple-element.34.after), calls=%async_computation.6 | async-start | bytes 131072 | tf_op jit(solution)/shard_map/all_to_all | solution.py:337
  135.5 4.0 %kernel_one.2 = (bf16[512,1024]{1,0:T(8,128)(2,1)S(1)}, f32[8,1,512]{2,1,0:T(1,128)S(1)}) custom-call(bf16[16,4,16,1024]{3,2,1,0:T(8,128)(2,1)} %bitcast.3, bf16[1024,1024]{1,0:T(8,128)(2,1)} %block.5, f32[16,1,1024]{2,1,0:T(1,128)} %get-tuple-element.34.after), custom_call_target="tpu_custom_call" | custom-call | flops 1073741824 | bytes 4194304 | tf_op jit(solution)/shard_map/kernel_one/pallas_call | solution.py:28
  139.5 2.4 %all-to-all-done.6 = f32[16,1,1024]{2,1,0:T(1,128)S(1)} async-done(((f32[16,1,1024]{2,1,0:T(1,128)}), f32[16,1,1024]{2,1,0:T(1,128)S(1)}, u32[]{:S(2)}, u32[]{:S(2)}) %all-to-all-start.6) | async-done | bytes 65568 | tf_op jit(solution)/shard_map/all_to_all | solution.py:337
  142.6 3.6 %all-to-all-start.7 = ((f32[4,1,1024]{2,1,0:T(1,128)}), f32[4,1,1024]{2,1,0:T(1,128)S(1)}, u32[]{:S(2)}, u32[]{:S(2)}) async-start(f32[4,1,1024]{2,1,0:T(1,128)} %broadcast_in_dim.10.after), calls=%async_computation.7 | async-start | bytes 32768 | tf_op jit(solution)/shard_map/all_to_all | solution.py:342
  146.2 4.0 %kernel_one.3 = (bf16[512,1024]{1,0:T(8,128)(2,1)S(1)}, f32[8,1,512]{2,1,0:T(1,128)S(1)}) custom-call(bf16[16,4,16,1024]{3,2,1,0:T(8,128)(2,1)} %bitcast.4, bf16[1024,1024]{1,0:T(8,128)(2,1)} %block.5, f32[4,1,1024]{2,1,0:T(1,128)} %broadcast_in_dim.10.after), custom_call_target="tpu_custom_call" | custom-call | flops 1073741824 | bytes 4194304 | tf_op jit(solution)/shard_map/kernel_one/pallas_call | solution.py:28
  151.2 6.5 %all-to-all-done.7.cols = f32[4,1,1024]{2,1,0:T(1,128)S(1)} async-done(((f32[4,1,1024]{2,1,0:T(1,128)}), f32[4,1,1024]{2,1,0:T(1,128)S(1)}, u32[]{:S(2)}, u32[]{:S(2)}) %all-to-all-start.7) | async-done | bytes 16416 | tf_op jit(solution)/shard_map/all_to_all | solution.py:342
  158.4 10.5 %all_to_all.61.gathered = f32[8,2,1024]{2,1,0:T(2,128)S(1)} all-to-all(f32[8,2,1024]{2,1,0:T(2,128)S(1)} %rows.3), channel_id=1, replica_groups=mesh['x'=4,'z_hi'=4,'y'=4,'z_lo'=4,'core'=2] {'z_lo','core'}, dimensions={0} | all-to-all | bytes 131072 | tf_op jit(solution)/shard_map/all_to_all | solution.py:321
  169.8 11.1 %all_to_all.62 = f32[16,2,1024]{2,1,0:T(2,128)S(1)} all-to-all(f32[16,2,1024]{2,1,0:T(2,128)S(1)} %get-tuple-element.42), channel_id=1, replica_groups=mesh['x'=4,'z_hi'=4,'y'=4,'z_lo'=4,'core'=2] {'x','y'}, dimensions={0} | all-to-all | bytes 262144 | tf_op jit(solution)/shard_map/all_to_all | solution.py:337
  181.0 15.4 %all_to_all.63.cols = f32[4,2,1024]{2,1,0:T(2,128)S(1)} all-to-all(f32[4,2,1024]{2,1,0:T(2,128)S(1)} %broadcast_in_dim.11), channel_id=1, replica_groups=mesh['x'=4,'z_hi'=4,'y'=4,'z_lo'=4,'core'=2] {'z_hi'}, dimensions={0} | all-to-all | bytes 65536 | tf_op jit(solution)/shard_map/all_to_all | solution.py:342
  198.0 1.9 transport.1
  200.0 5.6 %collective-permute-start = (bf16[1040,512]{1,0:T(8,128)(2,1)S(1)}, bf16[1040,512]{1,0:T(8,128)(2,1)S(1)}, u32[]{:S(2)}, u32[]{:S(2)}) collective-permute-start(bf16[1040,512]{1,0:T(8,128)(2,1)S(1)} %get-tuple-element.45), channel_id=1, source_target_pairs={{0,1},{1,0},{2,3},{3,2},{4,5},{5,4},{6,7},{7,6},{8,9},{9,8},{10,11... | collective-permute-start | bytes 3194888 | tf_op jit(solution)/shard_map/ppermute | solution.py:366
  208.3 2.4 collective-permute-start.2
  210.7 2.9 %collective-permute-start.1 = (bf16[1024,128]{1,0:T(8,128)(2,1)S(1)}, bf16[1024,128]{1,0:T(8,128)(2,1)S(1)}, u32[]{:S(2)}, u32[]{:S(2)}) collective-permute-start(bf16[1024,128]{1,0:T(8,128)(2,1)S(1)} %get-tuple-element.48), channel_id=1, source_target_pairs={{0,2},{2,0},{4,6},{6,4},{1,3},{3,1},{5,7},{7,5},{8,10},{10,8},{12,... | collective-permute-start | bytes 786440 | tf_op jit(solution)/shard_map/ppermute | solution.py:386
  213.6 4.2 %collective-permute-done.2.came = bf16[1040,128]{1,0:T(8,128)(2,1)S(1)} collective-permute-done((bf16[1040,128]{1,0:T(8,128)(2,1)S(1)}, bf16[1040,128]{1,0:T(8,128)(2,1)S(1)}, u32[]{:S(2)}, u32[]{:S(2)}) %collective-permute-start.2) | collective-permute-done | bytes 266272 | tf_op jit(solution)/shard_map/ppermute | solution.py:385
  217.9 2.1 collective-permute-start.3
  220.6 2.8 %collective-permute-done.1.beside = bf16[1024,128]{1,0:T(8,128)(2,1)S(1)} collective-permute-done((bf16[1024,128]{1,0:T(8,128)(2,1)S(1)}, bf16[1024,128]{1,0:T(8,128)(2,1)S(1)}, u32[]{:S(2)}, u32[]{:S(2)}) %collective-permute-start.1) | collective-permute-done | bytes 262176 | tf_op jit(solution)/shard_map/ppermute | solution.py:386
  223.4 10.4 %collective-permute-done.3.far = bf16[1040,128]{1,0:T(8,128)(2,1)S(1)} collective-permute-done((bf16[1040,128]{1,0:T(8,128)(2,1)S(1)}, bf16[1040,128]{1,0:T(8,128)(2,1)S(1)}, u32[]{:S(2)}, u32[]{:S(2)}) %collective-permute-start.3) | collective-permute-done | bytes 266272 | tf_op jit(solution)/shard_map/ppermute | solution.py:388
  (30 shorter events, 13.7 us)
Async XLA Ops:
  7.2 128.3 %all-gather.3.cloned.1.call-start = ((), (), s32[]{:S(2)}) async-start(), calls=%async_computation.11 | async-start | bytes 2228224 | tf_op jit(solution)/shard_map/all_gather | solution.py:281
  132.0 10.0 %all-to-all-start.6 = ((f32[16,1,1024]{2,1,0:T(1,128)}), f32[16,1,1024]{2,1,0:T(1,128)S(1)}, u32[]{:S(2)}, u32[]{:S(2)}) async-start(f32[16,1,1024]{2,1,0:T(1,128)} %get-tuple-element.34.after), calls=%async_computation.6 | async-start | bytes 131072 | tf_op jit(solution)/shard_map/all_to_all | solution.py:337
  142.6 15.1 %all-to-all-start.7 = ((f32[4,1,1024]{2,1,0:T(1,128)}), f32[4,1,1024]{2,1,0:T(1,128)S(1)}, u32[]{:S(2)}, u32[]{:S(2)}) async-start(f32[4,1,1024]{2,1,0:T(1,128)} %broadcast_in_dim.10.after), calls=%async_computation.7 | async-start | bytes 32768 | tf_op jit(solution)/shard_map/all_to_all | solution.py:342
  150.2 1.0 copy-start.1
  157.7 11.1 %copy-start.2 = (bf16[512,1024]{1,0:T(8,128)(2,1)S(1)}, bf16[512,1024]{1,0:T(8,128)(2,1)}, u32[]{:S(2)}) copy-start(bf16[512,1024]{1,0:T(8,128)(2,1)} %copy-done.1) | copy-start | bytes 3145732
  196.4 1.6 copy-start
  200.0 7.9 %collective-permute-start = (bf16[1040,512]{1,0:T(8,128)(2,1)S(1)}, bf16[1040,512]{1,0:T(8,128)(2,1)S(1)}, u32[]{:S(2)}, u32[]{:S(2)}) collective-permute-start(bf16[1040,512]{1,0:T(8,128)(2,1)S(1)} %get-tuple-element.45), channel_id=1, source_target_pairs={{0,1},{1,0},{2,3},{3,2},{4,5},{5,4},{6,7},{7,6},{8,9},{9,8},{10,11... | collective-permute-start | bytes 3194888 | tf_op jit(solution)/shard_map/ppermute | solution.py:366
  208.3 9.5 %collective-permute-start.2 = (bf16[1040,128]{1,0:T(8,128)(2,1)S(1)}, bf16[1040,128]{1,0:T(8,128)(2,1)S(1)}, u32[]{:S(2)}, u32[]{:S(2)}) collective-permute-start(bf16[1040,128]{1,0:T(8,128)(2,1)S(1)} %get-tuple-element.50), channel_id=1, source_target_pairs={{0,2},{2,0},{4,6},{6,4},{1,3},{3,1},{5,7},{7,5},{8,10},{10,8},{12,... | collective-permute-start | bytes 798728 | tf_op jit(solution)/shard_map/ppermute | solution.py:385
  210.7 12.8 %collective-permute-start.1 = (bf16[1024,128]{1,0:T(8,128)(2,1)S(1)}, bf16[1024,128]{1,0:T(8,128)(2,1)S(1)}, u32[]{:S(2)}, u32[]{:S(2)}) collective-permute-start(bf16[1024,128]{1,0:T(8,128)(2,1)S(1)} %get-tuple-element.48), channel_id=1, source_target_pairs={{0,2},{2,0},{4,6},{6,4},{1,3},{3,1},{5,7},{7,5},{8,10},{10,8},{12,... | collective-permute-start | bytes 786440 | tf_op jit(solution)/shard_map/ppermute | solution.py:386
  217.9 16.0 %collective-permute-start.3 = (bf16[1040,128]{1,0:T(8,128)(2,1)S(1)}, bf16[1040,128]{1,0:T(8,128)(2,1)S(1)}, u32[]{:S(2)}, u32[]{:S(2)}) collective-permute-start(bf16[1040,128]{1,0:T(8,128)(2,1)S(1)} %get-tuple-element.52), channel_id=1, source_target_pairs={{0,4},{4,0},{2,6},{6,2},{1,5},{5,1},{3,7},{7,3},{8,12},{12,8},{10,... | collective-permute-start | bytes 798728 | tf_op jit(solution)/shard_map/ppermute | solution.py:388
Sparse Core Ops, SparseCore 0:
  66.9 62.7 all-gather.2
